TPU v7x, 128 devices: a whole 4x4x4 slice. The times are simulated.
128 devices in a mesh: region: 4 (over z_hi, core), dev: 32 (over x, y, z_lo).
Axes of the slice: x: 4, y: 4, z: 4 (z_hi: 2, z_lo: 2; z = z_hi * 2 + z_lo), core: 2. Of those that a mesh axis runs over, the one named last changes fastest.
Arguments:
- science: float32 [4, 32, 2, 1024, 2, 128], P('region', 'dev'), may hold values from -6 to 6, as said below
- coadd: float32 [4, 4096, 2, 128], P('region', 'dev'), may hold values from -6 to 6, as said below
- coefficients: float32 [4, 32, 2, 31, 3], P('region', 'dev'), may hold values from -1 to 1
- strip_start: int32 [4, 32, 2], P('region', 'dev'), may hold values from 0 to 24, as said below
Outputs:
- patch_sums: float32 [4, 4096, 2, 128], P('region', 'dev')
Inputs may be any that keep to these rules, and one draw needn't show every extreme that they name: Strip e of a device covers blocks strip_start .. strip_start + 7 of its region; the two strips of one device cover 2 * 8 different blocks; no block is covered by more than 32 strips, and in every region some block is covered by a strip of every device of the region; some region has a strip starting at 0 and some region one starting at 24. `science`: plane 1 holds positive variances. `coadd`: plane 1 holds positive variances.
All inputs are finite; a program needn't handle non-finite values.
Results may differ from a plain program's by a relative error of at most 0.0001.
Values sent between devices are 32-bit elements; how exact they have to be, the bound alone decides.
A program may use at most 64 MiB of HBM per device.

v0:
```python
import jax
import jax.numpy as jnp
from jax import lax
from jax.sharding import PartitionSpec as P

BLK = 128
CW = 128
EXP_DEV = 2
KSIZE = 21
NPROF = 12


SPREADS = (1.0, 2.0, 4.0)
DEGREES = (4, 3, 2)


def padded_2(cells, sides, width):
    for axis, dim in sides:
        count = lax.axis_size(axis)
        ends = count - 1
        head = lax.slice_in_dim(cells, 0, width, axis=dim)
        tail = lax.slice_in_dim(cells, cells.shape[dim] - width, cells.shape[dim], axis=dim)
        cells = jnp.concatenate(
            [
                lax.ppermute(tail, axis, [(i, (i + 1) % count) for i in range(ends)]),
                cells,
                lax.ppermute(head, axis, [((i + 1) % count, i) for i in range(ends)]),
            ],
            axis=dim,
        )
    return cells


def profile_values(offset, spread, exponent):
    half_width = (KSIZE - 1) // 2
    scaled = offset / half_width
    return scaled**exponent * jnp.exp(-offset * offset / (2.0 * spread * spread))


def profile_list():
    entries = []
    for spread, degree in zip(SPREADS, DEGREES):
        for exponent in range(degree + 1):
            entries.append((spread, exponent))
    return entries


def profile_norms():
    taps = jnp.arange(KSIZE, dtype=jnp.float32) - (KSIZE - 1) // 2
    return [
        jnp.sum(jnp.abs(profile_values(taps, spread, exponent)))
        for spread, exponent in profile_list()
    ]


def basis_list():
    listing = []
    offset = 0
    for degree in DEGREES:
        for vertical in range(degree + 1):
            for across in range(degree + 1 - vertical):
                listing.append((offset + vertical, offset + across))
        offset = offset + degree + 1
    return listing


def across_matrix(norm_values):
    half_width = (KSIZE - 1) // 2
    source = jnp.arange(CW, dtype=jnp.float32)[:, None]
    target = jnp.arange(CW, dtype=jnp.float32)[None, :]
    offset = source - target
    inside = jnp.abs(offset) <= half_width
    blocks = []
    for (spread, exponent), norm_value in zip(profile_list(), norm_values):
        blocks.append(jnp.where(inside, profile_values(offset, spread, exponent) / norm_value, 0.0))
    return jnp.concatenate(blocks, axis=1)


def down_matrix(spread, exponent, norm_value, out_rows):
    half_width = (KSIZE - 1) // 2
    output_rows = jnp.arange(out_rows, dtype=jnp.float32)[:, None]
    input_rows = jnp.arange(out_rows + 2 * half_width, dtype=jnp.float32)[None, :]
    offset = input_rows - output_rows - half_width
    inside = jnp.abs(offset) <= half_width
    return jnp.where(inside, profile_values(offset, spread, exponent) / norm_value, 0.0)


def kernel_norm_list(profile_sums):
    return jnp.stack(
        [profile_sums[upright] * profile_sums[across] for upright, across in basis_list()]
    )


def strip_terms(window, strip_data, spatial_terms, wide_matrix, norm_values, profile_sums):
    half_width = (KSIZE - 1) // 2
    out_rows = strip_data.shape[0]
    block_count = out_rows // BLK
    listing = basis_list()
    flux_plane = window[:, 0, :]
    in_rows = flux_plane.shape[0]
    across_all = jnp.dot(flux_plane, wide_matrix, precision=lax.Precision.HIGHEST).reshape(
        in_rows, NPROF, CW
    )
    column_coords = (2.0 * jnp.arange(CW, dtype=jnp.float32) + 1.0) / CW - 1.0
    row_coords = (2.0 * jnp.arange(out_rows, dtype=jnp.float32) + 1.0) / out_rows - 1.0
    row_blocks = row_coords.reshape(block_count, BLK, 1)
    model_blocks = jnp.zeros((block_count, BLK, CW), jnp.float32)
    for vertical, (spread, exponent) in enumerate(profile_list()):
        flat_part = jnp.zeros((in_rows, CW), jnp.float32)
        sloped = jnp.zeros((in_rows, CW), jnp.float32)
        for number, (upright, across) in enumerate(listing):
            if upright == vertical:
                flat_part = (
                    flat_part
                    + (spatial_terms[number, 0] + spatial_terms[number, 1] * column_coords[None, :])
                    * across_all[:, across, :]
                )
                sloped = sloped + spatial_terms[number, 2] * across_all[:, across, :]
        paired = jnp.stack([flat_part, sloped])
        pieces = jnp.stack(
            [
                paired[:, block_index * BLK : block_index * BLK + BLK + 2 * half_width]
                for block_index in range(block_count)
            ],
            axis=1,
        )
        matrix_rows = down_matrix(spread, exponent, norm_values[vertical], BLK)
        smoothed = jnp.einsum("oi,tbic->tboc", matrix_rows, pieces, precision=lax.Precision.HIGHEST)
        model_blocks = model_blocks + smoothed[0] + row_blocks * smoothed[1]
    model_image = model_blocks.reshape(out_rows, CW)
    kernel_norms = kernel_norm_list(profile_sums)
    kernel_sum = (
        jnp.sum(spatial_terms[:, 0] * kernel_norms)
        + jnp.sum(spatial_terms[:, 1] * kernel_norms) * column_coords[None, :]
        + jnp.sum(spatial_terms[:, 2] * kernel_norms) * row_coords[:, None]
    )
    variance = (
        strip_data[:, 1, :]
        + kernel_sum * kernel_sum * window[half_width : half_width + out_rows, 1, :]
    )
    weight = 1.0 / variance
    return jnp.stack([(strip_data[:, 0, :] - model_image) * weight, weight], axis=1)


def per_device(science, coadd, coefficients, strip_start):
    half_width = (KSIZE - 1) // 2
    strip_rows = science.shape[3]
    groups = lax.axis_size("dev")
    norm_values = profile_norms()
    taps = jnp.arange(KSIZE, dtype=jnp.float32) - half_width
    profile_sums = jnp.stack(
        [
            jnp.sum(profile_values(taps, spread, exponent)) / norm_value
            for (spread, exponent), norm_value in zip(profile_list(), norm_values)
        ]
    )
    wide_matrix = across_matrix(norm_values)
    region_band = lax.all_gather(coadd[0], "dev", axis=0, tiled=True)
    edge_rows = jnp.concatenate([region_band[:half_width], region_band[-half_width:]], axis=0)
    extended = padded_2(edge_rows, (("region", 0),), half_width)
    padded = jnp.concatenate([extended[:half_width], region_band, extended[-half_width:]], axis=0)
    dense_sums = jnp.zeros((groups * BLK, 2, CW), jnp.float32)
    for strip_number in range(EXP_DEV):
        first_row = strip_start[0, 0, strip_number] * BLK
        window = lax.dynamic_slice_in_dim(padded, first_row, strip_rows + 2 * half_width, 0)
        contributions = strip_terms(
            window,
            science[0, 0, strip_number],
            coefficients[0, 0, strip_number],
            wide_matrix,
            norm_values,
            profile_sums,
        )
        current = lax.dynamic_slice_in_dim(dense_sums, first_row, strip_rows, 0)
        dense_sums = lax.dynamic_update_slice_in_dim(
            dense_sums, current + contributions, first_row, 0
        )
    result = lax.psum_scatter(dense_sums, "dev", scatter_dimension=0, tiled=True)
    return result[None]


def solution(mesh):
    placed = (
        P("region", "dev", None, None, None, None),
        P("region", "dev", None, None),
        P("region", "dev", None, None, None),
        P("region", "dev", None),
    )
    return jax.shard_map(
        per_device,
        mesh=mesh,
        in_specs=placed,
        out_specs=P("region", "dev", None, None),
        check_vma=False,
    )
```

profile of v0, /device:TPU:0, one launch (start us, length us, event | category | flops | bytes accessed | tf_op | source)
XLA Modules:
  0.0 491.9 jit_solution(11164558315770203030)
XLA Ops:
  136.1 33.3 %all-gather.3.cloned.1.call-done = f32[1,4096,2,128]{3,1,2,0:T(8,128)} async-done(((f32[1,128,2,128]{3,1,2,0:T(8,128)}), f32[1,4096,2,128]{3,1,2,0:T(8,128)}) %all-gather.3.cloned.1.call-update) | async-done | bytes 4194320 | tf_op jit(solution)/shard_map/all_gather | solution.py:158
  175.2 4.0 collective-permute-done.1
  179.2 13.4 %concatenate.6 = f32[4116,2,128]{2,0,1:T(8,128)} concatenate(f32[10,2,128]{2,0,1:T(8,128)S(1)} %collective-permute-done, f32[4096,2,128]{2,0,1:T(8,128)} %bitcast.1688, f32[10,2,128]{2,0,1:T(8,128)S(1)} %collective-permute-done.1), dimensions={0} | concatenate | bytes 8429568 | tf_op jit(solution)/shard_map/concatenate | solution.py:161
  192.6 6.2 %fusion.25 = f32[1044,12,128]{2,0,1:T(8,128)S(1)} fusion(f32[12,128,128]{2,1,0:T(8,128)S(1)} %bitcast.1689, f32[4116,2,128]{2,0,1:T(8,128)} %concatenate.6, s32[]{:T(128)S(6)} %select_n.126), kind=kOutput, calls=%fused_computation.402 | convolution fusion | flops 2463105024 | bytes 7737348 | tf_op jit(solution)/shard_map/dot_general | solution.py:101
  198.8 6.5 %fusion.26 = f32[1044,12,128]{2,0,1:T(8,128)S(1)} fusion(f32[12,128,128]{2,1,0:T(8,128)S(1)} %bitcast.1690, f32[4116,2,128]{2,0,1:T(8,128)} %concatenate.6, s32[]{:T(128)S(6)} %select_n.99), kind=kOutput, calls=%fused_computation.416 | convolution fusion | flops 2463105024 | bytes 7737348 | tf_op jit(solution)/shard_map/dot_general | solution.py:101
  205.3 2.2 multiply_add_fusion.17
  207.5 5.6 %multiply_add_fusion.16 = (f32[1,1044,128]{2,1,0:T(8,128)S(1)}, f32[1,1044,128]{2,1,0:T(8,128)S(1)}, f32[1,1044,128]{2,1,0:T(8,128)S(1)}, f32[1,1044,128]{2,1,0:T(8,128)S(1)}) fusion(f32[1044,12,128]{2,0,1:T(8,128)S(1)} %fusion.25, f32[]{:T(128)} %bitcast.317, f32[]{:T(128)} %bitcast.316, f32[]{:T(128)} %bitcast.315, f32[]{:T(128)} %bitcast.314, ...), kind=kLoop, calls=%fused_computation.433 | loop fusion | flops 1870848 | bytes 5345316 | tf_op jit(solution)/shard_map/add | solution.py:118
  213.3 2.1 convolution_bitcast_fusion.11
  215.5 2.2 multiply_add_fusion.15
  217.6 5.8 %multiply_add_fusion.14 = (f32[1,1044,128]{2,1,0:T(8,128)S(1)}, f32[1,1044,128]{2,1,0:T(8,128)S(1)}, f32[1,1044,128]{2,1,0:T(8,128)S(1)}) fusion(f32[1044,12,128]{2,0,1:T(8,128)S(1)} %fusion.25, f32[]{:T(128)} %bitcast.341, f32[]{:T(128)} %bitcast.340, f32[]{:T(128)} %bitcast.339, f32[]{:T(128)} %bitcast.338, f32[]{:T(128)} %bitcast.362, f32[]{:T(128)} %bitcast.361, ...), kind=kLoop, calls=%fused_computation.431 | loop fusion | flops 2004480 | bytes 4810788 | tf_op jit(solution)/shard_map/add | solution.py:118
  225.4 2.1 multiply_add_fusion.13
  229.5 2.7 multiply_add_fusion.11
  232.4 1.8 convolution_bitcast_fusion.8
  238.8 1.8 convolution_bitcast_fusion.5
  240.8 1.8 convolution_bitcast_fusion.4
  243.3 1.8 convolution_bitcast_fusion.3
  251.2 2.1 multiply_add_fusion.35
  253.3 5.9 %multiply_add_fusion.34 = (f32[1,1044,128]{2,1,0:T(8,128)S(1)}, f32[1,1044,128]{2,1,0:T(8,128)S(1)}, f32[1,1044,128]{2,1,0:T(8,128)S(1)}, f32[1,1044,128]{2,1,0:T(8,128)S(1)}) fusion(f32[1044,12,128]{2,0,1:T(8,128)S(1)} %fusion.26, f32[]{:T(128)} %bitcast.28, f32[]{:T(128)} %bitcast.27, f32[]{:T(128)} %bitcast.26, f32[]{:T(128)} %bitcast.25, f32[]{:T(128)} %bitcast.24, ...), kind=kLoop, calls=%fused_computation.451 | loop fusion | flops 1870848 | bytes 5345316 | tf_op jit(solution)/shard_map/add | solution.py:118
  259.4 1.8 convolution_bitcast_fusion.23
  261.3 2.3 multiply_add_fusion.33
  263.6 5.9 %multiply_add_fusion.32 = (f32[1,1044,128]{2,1,0:T(8,128)S(1)}, f32[1,1044,128]{2,1,0:T(8,128)S(1)}, f32[1,1044,128]{2,1,0:T(8,128)S(1)}) fusion(f32[1044,12,128]{2,0,1:T(8,128)S(1)} %fusion.26, f32[]{:T(128)} %bitcast.54, f32[]{:T(128)} %bitcast.53, f32[]{:T(128)} %bitcast.52, f32[]{:T(128)} %bitcast.51, f32[]{:T(128)} %bitcast.76, f32[]{:T(128)} %bitcast.75, ...), kind=kLoop, calls=%fused_computation.449 | loop fusion | flops 2004480 | bytes 4810788 | tf_op jit(solution)/shard_map/add | solution.py:118
  271.5 2.0 multiply_add_fusion.31
  275.6 2.8 multiply_add_fusion.29
  278.6 2.0 convolution_bitcast_fusion.20
  281.1 1.8 convolution_bitcast_fusion.19
  285.2 1.8 convolution_bitcast_fusion.17
  289.3 1.8 convolution_bitcast_fusion.15
  301.2 3.2 fusion.32
  304.4 2.2 broadcast_in_dim.46
  307.7 2.7 fusion.29
  310.4 2.3 fusion.24
  312.8 170.4 %reduce-scatter.2.cloned.1.call-done = f32[128,2,128]{2,0,1:T(8,128)} async-done(((f32[4096,2,128]{2,0,1:T(8,128)}), f32[128,2,128]{2,0,1:T(8,128)}) %reduce-scatter.2.cloned.1.call-update) | async-done | bytes 131088 | tf_op jit(solution)/shard_map/reduce_scatter | solution.py:178
  (364 shorter events, 154.9 us)
Async XLA Ops:
  6.5 120.4 %copy-start.1 = (s32[1,1,2]{2,1,0:T(1,128)S(1)}, s32[1,1,2]{2,1,0:T(1,128)}, u32[]{:S(2)}) copy-start(s32[1,1,2]{2,1,0:T(1,128)} %param.7) | copy-start | bytes 28
  6.5 129.2 %copy-start = (f32[1,1,2,1024,2,128]{5,4,3,2,1,0:T(2,128)S(1)}, f32[1,1,2,1024,2,128]{5,4,3,2,1,0:T(2,128)}, u32[]{:S(2)}) copy-start(f32[1,1,2,1024,2,128]{5,4,3,2,1,0:T(2,128)} %param.4) | copy-start | bytes 6291460
  6.5 162.8 %all-gather.3.cloned.1.call-start = ((), (), s32[]{:S(2)}) async-start(), calls=%async_computation.2 | async-start | bytes 4325376 | tf_op jit(solution)/shard_map/all_gather | solution.py:158
  8.3 474.9 %reduce-scatter.2.cloned.1.call-start = ((), (), s32[]{:S(2)}) async-start(), calls=%async_computation.1 | async-start | bytes 4325376 | tf_op jit(solution)/shard_map/reduce_scatter | solution.py:178
  170.1 5.1 %collective-permute-start = (f32[10,2,128]{2,0,1:T(8,128)S(1)}, f32[10,2,128]{2,0,1:T(8,128)S(1)}, u32[]{:S(2)}, u32[]{:S(2)}) collective-permute-start(f32[10,2,128]{2,0,1:T(8,128)S(1)} %get-tuple-element.67), channel_id=1, source_target_pairs={{0,32},{32,64},{64,96},{1,33},{33,65},{65,97},{2,34},{34,66},{66,9... | collective-permute-start | bytes 30728 | tf_op jit(solution)/shard_map/ppermute | solution.py:25
  171.4 7.8 %collective-permute-start.1 = (f32[10,2,128]{2,0,1:T(8,128)S(1)}, f32[10,2,128]{2,0,1:T(8,128)S(1)}, u32[]{:S(2)}, u32[]{:S(2)}) collective-permute-start(f32[10,2,128]{2,0,1:T(8,128)S(1)} %get-tuple-element.66), channel_id=1, source_target_pairs={{32,0},{64,32},{96,64},{33,1},{65,33},{97,65},{34,2},{66,34},{98,6... | collective-permute-start | bytes 30728 | tf_op jit(solution)/shard_map/ppermute | solution.py:27
Sparse Core Ops, SparseCore 0:
  9.0 160.3 all-gather.2
  312.9 170.1 reduce-scatter.1
where the time goes:
time: 498 us; the launch traced here: 492 us
  waiting for transfers between devices  208 us (42%)
  other arithmetic  159 us (32%)
  matrix products  55.8 us (11%)
  local copies, waits for them, and re-layouts  34.5 us (7%)
  between operations  32.5 us (7%)
    reduce_scatter x1, waiting for transfers between devices, per_device(): lax.psum_scatter(dense_sums, 'dev', scatter_dimension=0, tiled=True)  170 us
    add x62, other arithmetic, strip_terms(): spatial_terms[number, 0] + spatial_terms[number, 1] * column_coords[None, :]  78 us
    dot_general x24, matrix products, strip_terms(): jnp.einsum('oi,tbic->tboc', matrix_rows, pieces, precision=lax.Precision....  43.2 us
    all_gather x1, waiting for transfers between devices, per_device(): region_band = lax.all_gather(coadd[0], 'dev', axis=0, tiled=True)  33.3 us
    add x4, other arithmetic, strip_terms(): sloped = sloped + spatial_terms[number, 2] * across_all[:, across, :]  23.3 us
    add x8, other arithmetic, strip_terms(): flat_part + (spatial_terms[number, 0] + spatial_terms[number, 1] * column...  18.4 us
    concatenate x1, local copies, waits for them, and re-layouts, per_device(): jnp.concatenate([extended[:half_width], region_band, extended[-half_width...  13.4 us
    dot_general x2, matrix products, strip_terms(): jnp.dot(flux_plane, wide_matrix, precision=lax.Precision.HIGHEST)  12.7 us
  transfers between devices with their start and end apart: 4, of which 3 were waited for; matrix products, arithmetic and copies ran while one was open for 23% of the time, Pallas kernels for 0%

commit v1 on v0

v1 whole, which is shorter than its diff:
```python
import jax
import jax.numpy as jnp
import ml_dtypes
import numpy as np
from jax import lax
from jax.experimental import pallas as pl
from jax.experimental.pallas import tpu as pltpu
from jax.sharding import PartitionSpec as P

BLK = 128
CW = 128
KSIZE = 21
NPROF = 12
NBASIS = 31
SPREADS = (1.0, 2.0, 4.0)
DEGREES = (4, 3, 2)

RES = 8
NX = 4
EDGE = 16
EXT = BLK + 2 * EDGE
DEPTH = 512
HALF = BLK // 2
F32 = jnp.float32
BF16 = jnp.bfloat16
MESH = pl.DeviceIdType.MESH


def basis_list():
    listing = []
    offset = 0
    for degree in DEGREES:
        for vertical in range(degree + 1):
            for across in range(degree + 1 - vertical):
                listing.append((offset + vertical, offset + across))
        offset = offset + degree + 1
    return listing


BASIS = basis_list()


def profiles():
    half_width = (KSIZE - 1) // 2
    taps = np.arange(KSIZE, dtype=np.float64) - half_width
    rows = []
    for spread, degree in zip(SPREADS, DEGREES):
        for exponent in range(degree + 1):
            values = (taps / half_width) ** exponent * np.exp(-taps * taps / (2.0 * spread * spread))
            rows.append(values / np.abs(values).sum())
    return np.stack(rows)


def split_np(matrix):
    high = matrix.astype(np.float32).astype(ml_dtypes.bfloat16)
    low = (matrix - high.astype(np.float64)).astype(np.float32).astype(ml_dtypes.bfloat16)
    return high, low


def constant_matrices():
    half_width = (KSIZE - 1) // 2
    prof = profiles()
    wide = np.zeros((CW, NPROF, CW))
    for target in range(CW):
        for tap in range(KSIZE):
            source = target + tap - half_width
            if 0 <= source < CW:
                wide[source, :, target] = prof[:, tap]
    high, low = split_np(wide.reshape(CW, NPROF // 2, 2 * CW).transpose(1, 0, 2))
    across = np.concatenate([high, high, low], axis=1)
    tall = np.zeros((NPROF, BLK, EXT))
    for target in range(BLK):
        for tap in range(KSIZE):
            tall[:, target, EDGE + target + tap - half_width] = prof[:, tap]
    high, low = split_np(tall)
    pad = np.zeros((NPROF, BLK, DEPTH - 3 * EXT), ml_dtypes.bfloat16)
    down = np.concatenate([high, low, high, pad], axis=2).reshape(NPROF * BLK, DEPTH)
    sums = prof.sum(axis=1)
    norms = np.zeros((1, CW), np.float32)
    for number, (vertical, horizontal) in enumerate(BASIS):
        norms[0, number] = sums[vertical] * sums[horizontal]
    return across, down, norms


def kernel(
    regions,
    sci_hbm, sky_hbm, coef_ref, start_ref, across_hbm, down_hbm, norm_ref,
    out_ref,
    sci, pack, recv, sky, edge, across, down, wide, basis, skyvar,
    acc, part, tab, tabs, num, nums, tab_s, num_s,
    loc_sem, sky_ss, sky_rs, edge_ss, edge_rs, fwd_ss, fwd_rs,
    tab_ss, tab_rs, num_ss, num_rs, sci_ss, sci_rs, red_ss, red_rs,
):
    region = lax.axis_index("region")
    dev = lax.axis_index("dev")
    x = dev // RES
    r = dev % RES
    y = r // 2
    z = r % 2
    total_devs = regions * RES * NX
    whole = region * (RES * NX) + dev

    def peer(t):
        return ((y + t // 2) % 4) * 2 + (z + t % 2) % 2

    def giver(t):
        return ((y + 4 - t // 2) % 4) * 2 + (z + t % 2) % 2

    def plane_id(res):
        return {"dev": x * RES + res}

    def line_id(dx):
        return {"dev": ((x + dx) % NX) * RES + r}

    def sky_id(step):
        other = (whole + step + total_devs) % total_devs
        return {"region": other // (RES * NX), "dev": other % (RES * NX)}

    def sci_copy(h, t, slot):
        return pltpu.make_async_remote_copy(
            src_ref=pack.at[h, t], dst_ref=recv.at[h, slot],
            send_sem=sci_ss.at[h, t], recv_sem=sci_rs.at[h, slot],
            device_id=plane_id(peer(t)), device_id_type=MESH)

    def tab_copy(t, slot):
        return pltpu.make_async_remote_copy(
            src_ref=tab, dst_ref=tabs.at[slot],
            send_sem=tab_ss.at[t], recv_sem=tab_rs.at[slot],
            device_id=plane_id(peer(t)), device_id_type=MESH)

    def num_copy(t, slot):
        return pltpu.make_async_remote_copy(
            src_ref=num, dst_ref=nums.at[slot],
            send_sem=num_ss.at[t], recv_sem=num_rs.at[slot],
            device_id=plane_id(peer(t)), device_id_type=MESH)

    def sky_copy(dx, slot):
        return pltpu.make_async_remote_copy(
            src_ref=sky.at[x], dst_ref=sky.at[slot],
            send_sem=sky_ss.at[dx], recv_sem=sky_rs.at[slot],
            device_id=line_id(dx), device_id_type=MESH)

    def fwd_copy(dx, slot):
        return pltpu.make_async_remote_copy(
            src_ref=edge.at[x], dst_ref=edge.at[slot],
            send_sem=fwd_ss.at[dx], recv_sem=fwd_rs.at[slot],
            device_id=line_id(dx), device_id_type=MESH)

    def edge_copy(side):
        rows = pl.ds(2 * (BLK - EDGE), 2 * EDGE) if side == 0 else pl.ds(0, 2 * EDGE)
        return pltpu.make_async_remote_copy(
            src_ref=sky.at[x, rows], dst_ref=edge.at[x_of(side), side],
            send_sem=edge_ss.at[side], recv_sem=edge_rs.at[side],
            device_id=sky_id(1 if side == 0 else -1), device_id_type=MESH)

    def x_of(side):
        other = (whole + (1 if side == 0 else -1) + total_devs) % total_devs
        return (other % (RES * NX)) // RES

    def edge_arrival(side):
        rows = pl.ds(2 * (BLK - EDGE), 2 * EDGE) if side == 0 else pl.ds(0, 2 * EDGE)
        return pltpu.make_async_remote_copy(
            src_ref=sky.at[x, rows], dst_ref=edge.at[x, side],
            send_sem=edge_ss.at[side], recv_sem=edge_rs.at[side],
            device_id=sky_id(1 if side == 0 else -1), device_id_type=MESH)

    def red_copy(h, dx, slot):
        return pltpu.make_async_remote_copy(
            src_ref=acc.at[h, (x + dx) % NX], dst_ref=part.at[h, slot],
            send_sem=red_ss.at[h, dx], recv_sem=red_rs.at[h, slot],
            device_id=line_id(dx), device_id_type=MESH)

    sky_load = pltpu.make_async_copy(sky_hbm, sky.at[x], loc_sem.at[0])
    sky_load.start()
    sci_load = pltpu.make_async_copy(sci_hbm, sci, loc_sem.at[1])
    sci_load.start()
    across_load = pltpu.make_async_copy(across_hbm, across, loc_sem.at[2])
    across_load.start()
    down_load = pltpu.make_async_copy(down_hbm, down, loc_sem.at[3])
    down_load.start()

    barrier = pltpu.get_barrier_semaphore()

    def greet(t, carry):
        pl.semaphore_signal(barrier, inc=1, device_id=plane_id(peer(t)), device_id_type=MESH)
        return carry

    lax.fori_loop(1, RES, greet, 0)
    for dx in range(1, NX):
        pl.semaphore_signal(barrier, inc=1, device_id=line_id(dx), device_id_type=MESH)
    for step in (1, -1):
        pl.semaphore_signal(barrier, inc=1, device_id=sky_id(step), device_id_type=MESH)

    lanes = lax.broadcasted_iota(jnp.int32, (8, CW), 1)
    sublanes = lax.broadcasted_iota(jnp.int32, (8, CW), 0)
    tab[...] = jnp.zeros((8, CW), F32)
    for term in range(3):
        tab[2 * term : 2 * term + 2, 0:NBASIS] = coef_ref[term]
    raw = tab[...]
    weighted = jnp.sum(raw * norm_ref[...], axis=1, keepdims=True)
    tab[...] = jnp.where(lanes == NBASIS, weighted, raw)
    start0 = start_ref[0, 0]
    start1 = start_ref[0, 1]
    num[...] = jnp.where(lanes == 0, start0, start1) + 0 * sublanes
    tabs[r] = tab[...]
    nums[r] = num[...]

    sky_load.wait()
    pl.semaphore_wait(barrier, RES - 1 + NX - 1 + 2)

    for side in (0, 1):
        edge_copy(side).start()
    for dx in range(1, NX):
        sky_copy(dx, x).start()
    sci_load.wait()

    starts = (start0, start1)

    def chosen(h, res, e):
        block = lax.rem(res - starts[e] + 4 * RES, RES)
        return sci[e, block, h]

    for h in range(2):
        for e in range(2):
            recv[h, r, e] = chosen(h, r, e)

        def give(t, carry):
            for e in range(2):
                pack[h, t, e] = chosen(h, peer(t), e)
            sci_copy(h, t, r).start()
            if h == 0:
                tab_copy(t, r).start()
                num_copy(t, r).start()
            return carry

        lax.fori_loop(1, RES, give, 0)

    for side in (0, 1):
        edge_arrival(side).wait_recv()
    for dx in range(1, NX):
        fwd_copy(dx, x).start()

    acc[...] = jnp.zeros(acc.shape, F32)
    across_load.wait()
    down_load.wait()

    first = (whole == 0) | ((region == 0) & (r == 0))
    last = (region == regions - 1) & (r == RES - 1)

    def spread_across(block):
        top = edge[block, 0, pl.ds(0, EDGE, stride=2), :]
        low = edge[block, 1, pl.ds(0, EDGE, stride=2), :]
        top = jnp.where(first & (block == 0), 0.0, top)
        low = jnp.where(last & (block == NX - 1), 0.0, low)
        body = sky[block, pl.ds(0, BLK, stride=2), :]
        for h in range(2):
            skyvar[block, h] = sky[block, pl.ds(h * BLK + 1, HALF, stride=2), :]
        full = jnp.concatenate([top, body, low], axis=0)
        high = full.astype(BF16)
        rest = (full - high.astype(F32)).astype(BF16)
        lhs = jnp.concatenate([high, rest, high], axis=1)
        return lhs

    for block in range(NX):
        @pl.when(block != x)
        def _():
            sky_copy(1, block).wait_recv()
            fwd_copy(1, block).wait_recv()

        lhs = spread_across(block)
        pair, side = block // 2, block % 2
        columns = slice(side * CW, (side + 1) * CW)

        def tile(q, carry):
            both = jnp.dot(lhs, across[q], preferred_element_type=F32)
            for half in range(2):
                values = both[:, half * CW : (half + 1) * CW]
                high = values.astype(BF16)
                rest = (values - high.astype(F32)).astype(BF16)
                profile = 2 * q + half
                wide[pair, profile, 0:EXT, columns] = high
                wide[pair, profile, EXT : 2 * EXT, columns] = high
                wide[pair, profile, 2 * EXT : 3 * EXT, columns] = rest
            return carry

        lax.fori_loop(0, NPROF // 2, tile, 0)

    for pair in range(2):
        for profile in range(NPROF):
            wide[pair, profile, 3 * EXT : DEPTH, :] = jnp.zeros((DEPTH - 3 * EXT, 2 * CW), BF16)

    def smooth(pair, carry):
        for across_profile in range(NPROF):
            users = [(k, v) for k, (v, a) in enumerate(BASIS) if a == across_profile]
            low_v = users[0][1]
            result = jnp.dot(
                down[low_v * BLK : (low_v + len(users)) * BLK, :],
                wide[pair, across_profile],
                preferred_element_type=F32)
            for place, (k, v) in enumerate(users):
                for side in range(2):
                    for h in range(2):
                        row = place * BLK + h * HALF
                        basis[2 * pair + side, k, h] = result[row : row + HALF, side * CW : (side + 1) * CW]
        return carry

    lax.fori_loop(0, 2, smooth, 0)

    def tables(t, carry):
        tab_copy(t, giver(t)).wait_recv()
        num_copy(t, giver(t)).wait_recv()
        return carry

    lax.fori_loop(1, RES, tables, 0)
    tab_move = pltpu.make_async_copy(tabs, tab_s, loc_sem.at[4])
    tab_move.start()
    num_move = pltpu.make_async_copy(nums, num_s, loc_sem.at[5])
    num_move.start()
    tab_move.wait()
    num_move.wait()

    xs = (2.0 * lanes.astype(F32) + 1.0) / CW - 1.0
    rows = (8 * lax.broadcasted_iota(jnp.int32, (8, 8, CW), 0)
            + lax.broadcasted_iota(jnp.int32, (8, 8, CW), 1)).astype(F32)
    ys_base = (2.0 * rows + 1.0) / (RES * BLK)

    def work(h, t):
        source = giver(t)
        found = []
        for e in range(2):
            start = num_s[source, 0, e]
            place = lax.rem(r - start + 4 * RES, RES)
            block = (start + place) // RES
            flat = jnp.zeros((8, 8, CW), F32)
            slope = jnp.zeros((8, 8, CW), F32)
            for k in range(NBASIS):
                image = basis[block, k, h].reshape(8, 8, CW)
                factor = tab_s[source, e, k] + tab_s[source, 2 + e, k] * xs
                flat = flat + factor[None] * image
                slope = slope + tab_s[source, 4 + e, k] * image
            y0 = (place * BLK + h * HALF).astype(F32)
            ys = ys_base + (y0 * (2.0 / (RES * BLK)) - 1.0)
            gain = (tab_s[source, e, NBASIS] + tab_s[source, 2 + e, NBASIS] * xs)[None] + tab_s[
                source, 4 + e, NBASIS] * ys
            flux = recv[h, source, e, pl.ds(0, HALF, stride=2), :].reshape(8, 8, CW)
            noise = recv[h, source, e, pl.ds(1, HALF, stride=2), :].reshape(8, 8, CW)
            behind = skyvar[block, h].reshape(8, 8, CW)
            weight = 1.0 / (noise + gain * gain * behind)
            diff = (flux - (flat + ys * slope)) * weight
            found.append((block, diff.reshape(HALF, CW), weight.reshape(HALF, CW)))
        for target in range(NX):
            for plane in range(2):
                span = slice(plane * HALF, (plane + 1) * HALF)
                old = acc[h, target, span, :]
                for block, diff, weight in found:
                    old = old + jnp.where(block == target, weight if plane else diff, 0.0)
                acc[h, target, span, :] = old

    for h in range(2):
        work(h, 0)

        def take(t, carry):
            sci_copy(h, t, giver(t)).wait_recv()
            work(h, t)
            return carry

        lax.fori_loop(1, RES, take, 0)
        for dx in range(1, NX):
            red_copy(h, dx, x).start()

    for h in range(2):
        for dx in range(1, NX):
            red_copy(h, dx, (x + dx) % NX).wait_recv()
        total = acc[h, x]
        for dx in range(1, NX):
            total = total + part[h, (x + dx) % NX]
        for plane in range(2):
            out_ref[pl.ds(h * BLK + plane, HALF, stride=2), :] = total[plane * HALF : (plane + 1) * HALF]

    for side in (0, 1):
        edge_copy(side).wait_send()
    for dx in range(1, NX):
        sky_copy(dx, x).wait_send()
        fwd_copy(dx, x).wait_send()
        for h in range(2):
            red_copy(h, dx, x).wait_send()

    def sent(t, carry):
        tab_copy(t, r).wait_send()
        num_copy(t, r).wait_send()
        for h in range(2):
            sci_copy(h, t, r).wait_send()
        return carry

    lax.fori_loop(1, RES, sent, 0)


def per_device(science, coadd, coefficients, strip_start):
    regions = lax.axis_size("region")
    across_np, down_np, norms_np = constant_matrices()
    sci = science.reshape(2, RES, 2, BLK, CW)
    sky = coadd.reshape(2 * BLK, CW)
    coef = jnp.transpose(coefficients[0, 0], (2, 0, 1))
    starts = strip_start[0]
    dma = pltpu.SemaphoreType.DMA
    scratch = [
        pltpu.VMEM((2, RES, 2, BLK, CW), F32),
        pltpu.VMEM((2, RES, 2, BLK, CW), F32),
        pltpu.VMEM((2, RES, 2, BLK, CW), F32),
        pltpu.VMEM((NX, 2 * BLK, CW), F32),
        pltpu.VMEM((NX, 2, 2 * EDGE, CW), F32),
        pltpu.VMEM(across_np.shape, BF16),
        pltpu.VMEM(down_np.shape, BF16),
        pltpu.VMEM((2, NPROF, DEPTH, 2 * CW), BF16),
        pltpu.VMEM((NX, NBASIS, 2, HALF, CW), F32),
        pltpu.VMEM((NX, 2, HALF, CW), F32),
        pltpu.VMEM((2, NX, BLK, CW), F32),
        pltpu.VMEM((2, NX, BLK, CW), F32),
        pltpu.VMEM((8, CW), F32),
        pltpu.VMEM((RES, 8, CW), F32),
        pltpu.VMEM((8, CW), jnp.int32),
        pltpu.VMEM((RES, 8, CW), jnp.int32),
        pltpu.SMEM((RES, 8, CW), F32),
        pltpu.SMEM((RES, 8, CW), jnp.int32),
        dma((6,)),
        dma((NX,)), dma((NX,)),
        dma((2,)), dma((2,)),
        dma((NX,)), dma((NX,)),
        dma((RES,)), dma((RES,)),
        dma((RES,)), dma((RES,)),
        dma((2, RES)), dma((2, RES)),
        dma((2, NX)), dma((2, NX)),
    ]
    hbm = pl.BlockSpec(memory_space=pl.ANY)
    vmem = pl.BlockSpec(memory_space=pltpu.VMEM)
    result = pl.pallas_call(
        lambda *refs: kernel(regions, *refs),
        out_shape=jax.ShapeDtypeStruct((2 * BLK, CW), F32),
        in_specs=[hbm, hbm, vmem, pl.BlockSpec(memory_space=pltpu.SMEM), hbm, hbm, vmem],
        out_specs=vmem,
        scratch_shapes=scratch,
        compiler_params=pltpu.CompilerParams(
            collective_id=0, has_side_effects=True, vmem_limit_bytes=52 * 1024 * 1024),
        cost_estimate=pl.CostEstimate(flops=3_000_000_000, bytes_accessed=6_000_000, transcendentals=0),
        name="difference_sums",
    )(sci, sky, coef, starts, jnp.asarray(across_np), jnp.asarray(down_np), jnp.asarray(norms_np))
    return result.reshape(1, BLK, 2, CW)


def solution(mesh):
    placed = (
        P("region", "dev", None, None, None, None),
        P("region", "dev", None, None),
        P("region", "dev", None, None, None),
        P("region", "dev", None),
    )
    return jax.shard_map(
        per_device,
        mesh=mesh,
        in_specs=placed,
        out_specs=P("region", "dev", None, None),
        check_vma=False,
    )
```

time: 498 us -> 46.5 us (0.09); the launches traced: 492 us -> 46.3 us
  waiting for transfers between devices: 208 us -> 0 us
  other arithmetic: 159 us -> 0 us
  matrix products: 55.8 us -> 0 us
  Pallas kernels: 0 us -> 41.5 us
  between operations: 32.5 us -> 0.01 us
  local copies, waits for them, and re-layouts: 34.5 us -> 4.82 us
    reduce_scatter x1 -> x0, waiting for transfers between devices: 170 us -> none  [per_device(): lax.psum_scatter(dense_sums, 'dev', scatter_dimension=0, tiled=True)]
    add x76 -> x0, other arithmetic: 122 us -> none  [the longest x62 78 us: strip_terms(): spatial_terms[number, 0] + spatial_terms[number, 1] * column_coords[None, :]]
    dot_general x26 -> x0, matrix products: 55.8 us -> none  [the longest x24 43.2 us: strip_terms(): jnp.einsum('oi,tbic->tboc', matrix_rows, pieces, precision=lax.Precision....]
    pallas_call x0 -> x1, Pallas kernels: none -> 41.5 us  [per_device(): pl.pallas_call(lambda *refs: kernel(regions, *refs), out_shape=jax.ShapeD...]
    all_gather x1 -> x0, waiting for transfers between devices: 33.3 us -> none  [per_device(): region_band = lax.all_gather(coadd[0], 'dev', axis=0, tiled=True)]
    slice x38 -> x0, local copies, waits for them, and re-layouts: 15.3 us -> none  [the longest x10 7.27 us: strip_terms(): sloped = sloped + spatial_terms[number, 2] * across_all[:, across, :]]
    reduce_sum x22 -> x0, other arithmetic: 14.3 us -> none  [the longest x12 7.86 us: profile_norms(): jnp.sum(jnp.abs(profile_values(taps, spread, exponent)))]
    concatenate x1 -> x0, local copies, waits for them, and re-layouts: 13.4 us -> none  [per_device(): jnp.concatenate([extended[:half_width], region_band, extended[-half_width...]
  transfers between devices with their start and end apart: 4 -> 0, of which waited for: 3 -> 0; matrix products, arithmetic and copies ran while one was open for 23% -> 0% of each run, Pallas kernels for 0% -> 0%
where the time goes in v1:
time: 46.5 us; the launch traced here: 46.3 us
  Pallas kernels  41.5 us (89%)
  local copies, waits for them, and re-layouts  4.82 us (10%)
    pallas_call x1, Pallas kernels, per_device(): pl.pallas_call(lambda *refs: kernel(regions, *refs), out_shape=jax.ShapeD...  41.5 us
    unnamed x11, local copies, waits for them, and re-layouts  4.82 us

profile of v1, /device:TPU:0, one launch (start us, length us, event | category | flops | bytes accessed | tf_op | source)
XLA Modules:
  0.0 46.3 jit_solution(14237444255372301628)
XLA Ops:
  0.0 0.0 copy-start
  0.0 0.9 %copy-done = f32[1,128,2,128]{3,2,1,0:T(2,128)S(1)} copy-done((f32[1,128,2,128]{3,2,1,0:T(2,128)S(1)}, f32[1,128,2,128]{3,2,1,0:T(2,128)}, u32[]{:S(2)}) %copy-start) | copy-done | bytes 131096
  0.9 0.0 copy-start.1
  0.9 0.7 %copy-done.1 = f32[1,1,2,31,3]{3,2,4,1,0:T(2,128)S(1)} copy-done((f32[1,1,2,31,3]{3,2,4,1,0:T(2,128)S(1)}, f32[1,1,2,31,3]{3,2,4,1,0:T(2,128)}, u32[]{:S(2)}) %copy-start.1) | copy-done | bytes 768
  1.6 0.0 copy-start.2
  1.6 0.7 %copy-done.2 = s32[1,1,2]{2,1,0:T(1,128)S(1)} copy-done((s32[1,1,2]{2,1,0:T(1,128)S(1)}, s32[1,1,2]{2,1,0:T(1,128)}, u32[]{:S(2)}) %copy-start.2) | copy-done | bytes 32
  2.2 0.0 copy-start.3
  2.2 1.3 %copy-done.3 = bf16[6,384,256]{2,1,0:T(8,128)(2,1)S(1)} copy-done((bf16[6,384,256]{2,1,0:T(8,128)(2,1)S(1)}, bf16[6,384,256]{2,1,0:T(8,128)(2,1)}, u32[]{:S(2)}) %copy-start.3) | copy-done | bytes 1179672
  3.5 0.0 copy-start.4
  3.5 0.7 %copy-done.4 = f32[1,128]{1,0:T(1,128)S(1)} copy-done((f32[1,128]{1,0:T(1,128)S(1)}, f32[1,128]{1,0:T(1,128)}, u32[]{:S(2)}) %copy-start.4) | copy-done | bytes 536
  4.2 41.5 %difference_sums.1 = f32[256,128]{1,0:T(8,128)S(1)} custom-call(f32[2,8,2,128,128]{4,3,2,1,0:T(8,128)} %bitcast.11, f32[256,128]{1,0:T(8,128)S(1)} %bitcast.8, f32[3,2,31]{2,1,0:T(2,128)S(1)} %bitcast.9, s32[1,2]{1,0:T(1,128)S(1)} %bitcast.10, bf16[6,384,256]{2,1,0:T(8,128)(2,1)S(1)} %copy-done.3, bf16[1536,512]{1,0:T(8,128)(2,1)} %constant.7.clone.refs_5_, ...), custom_call_target="tpu_custom_call" | custom-call | flops 3000000000 | bytes 6000000 | tf_op jit(solution)/shard_map/difference_sums/pallas_call | solution.py:436
  45.7 0.7 %copy.9 = f32[1,128,2,128]{3,2,1,0:T(2,128)} copy(f32[1,128,2,128]{3,2,1,0:T(2,128)S(1)} %bitcast.7) | data formatting | bytes 262144
Async XLA Ops:
  0.0 0.9 %copy-start = (f32[1,128,2,128]{3,2,1,0:T(2,128)S(1)}, f32[1,128,2,128]{3,2,1,0:T(2,128)}, u32[]{:S(2)}) copy-start(f32[1,128,2,128]{3,2,1,0:T(2,128)} %param.8) | copy-start | bytes 393220
  0.9 0.7 %copy-start.1 = (f32[1,1,2,31,3]{3,2,4,1,0:T(2,128)S(1)}, f32[1,1,2,31,3]{3,2,4,1,0:T(2,128)}, u32[]{:S(2)}) copy-start(f32[1,1,2,31,3]{3,2,4,1,0:T(2,128)} %param.9) | copy-start | bytes 2236
  1.6 0.7 %copy-start.2 = (s32[1,1,2]{2,1,0:T(1,128)S(1)}, s32[1,1,2]{2,1,0:T(1,128)}, u32[]{:S(2)}) copy-start(s32[1,1,2]{2,1,0:T(1,128)} %param.10) | copy-start | bytes 28
  2.2 1.3 %copy-start.3 = (bf16[6,384,256]{2,1,0:T(8,128)(2,1)S(1)}, bf16[6,384,256]{2,1,0:T(8,128)(2,1)}, u32[]{:S(2)}) copy-start(bf16[6,384,256]{2,1,0:T(8,128)(2,1)} %constant.6.clone.refs_4_) | copy-start | bytes 3538948
  3.5 0.7 %copy-start.4 = (f32[1,128]{1,0:T(1,128)S(1)}, f32[1,128]{1,0:T(1,128)}, u32[]{:S(2)}) copy-start(f32[1,128]{1,0:T(1,128)} %constant.8.clone.refs_6_) | copy-start | bytes 1540

commit v2 on v1

v2 whole, which is shorter than its diff:
```python
import jax
import jax.numpy as jnp
import ml_dtypes
import numpy as np
from jax import lax
from jax.experimental import pallas as pl
from jax.experimental.pallas import tpu as pltpu
from jax.sharding import PartitionSpec as P

BLK = 128
CW = 128
KSIZE = 21
NPROF = 12
NBASIS = 31
SPREADS = (1.0, 2.0, 4.0)
DEGREES = (4, 3, 2)

RES = 8
NX = 4
EDGE = 16
EXT = BLK + 2 * EDGE
DEPTH = 512
NQ = 4
PART = BLK // NQ
TILES = PART // 8
F32 = jnp.float32
BF16 = jnp.bfloat16
MESH = pl.DeviceIdType.MESH


def basis_list():
    listing = []
    offset = 0
    for degree in DEGREES:
        for vertical in range(degree + 1):
            for across in range(degree + 1 - vertical):
                listing.append((offset + vertical, offset + across))
        offset = offset + degree + 1
    return listing


BASIS = basis_list()


def profiles():
    half_width = (KSIZE - 1) // 2
    taps = np.arange(KSIZE, dtype=np.float64) - half_width
    rows = []
    for spread, degree in zip(SPREADS, DEGREES):
        for exponent in range(degree + 1):
            values = (taps / half_width) ** exponent * np.exp(-taps * taps / (2.0 * spread * spread))
            rows.append(values / np.abs(values).sum())
    return np.stack(rows)


def split_np(matrix):
    high = matrix.astype(np.float32).astype(ml_dtypes.bfloat16)
    low = (matrix - high.astype(np.float64)).astype(np.float32).astype(ml_dtypes.bfloat16)
    return high, low


def constant_matrices():
    half_width = (KSIZE - 1) // 2
    prof = profiles()
    wide = np.zeros((CW, NPROF, CW))
    for target in range(CW):
        for tap in range(KSIZE):
            source = target + tap - half_width
            if 0 <= source < CW:
                wide[source, :, target] = prof[:, tap]
    high, low = split_np(wide.reshape(CW, NPROF // 2, 2 * CW).transpose(1, 0, 2))
    across = np.concatenate([high, high, low], axis=1)
    tall = np.zeros((NPROF, BLK, EXT))
    for target in range(BLK):
        for tap in range(KSIZE):
            tall[:, target, (target + tap - half_width) % EXT] = prof[:, tap]
    high, low = split_np(tall)
    pad = np.zeros((NPROF, BLK, DEPTH - 3 * EXT), ml_dtypes.bfloat16)
    down = np.concatenate([high, low, high, pad], axis=2).reshape(NPROF * BLK, DEPTH)
    sums = prof.sum(axis=1)
    norms = np.zeros((8, CW), np.float32)
    for number, (vertical, horizontal) in enumerate(BASIS):
        norms[:, number] = sums[vertical] * sums[horizontal]
    return across, down, norms


def kernel(
    regions,
    sci_hbm, sky_hbm, coef_hbm, start_hbm, across_hbm, down_hbm, norm_hbm,
    out_ref,
    sci0, sci1, sci2, sci3, pack, recv, sky, edge, across, down, wide, basis, skyvar,
    acc, part, tab, tabs, num, nums, tab_s, num_s, coef_ref, start_ref, norm_ref,
    loc_sem, sky_ss, sky_rs, edge_ss, edge_rs, fwd_ss, fwd_rs,
    tab_ss, tab_rs, num_ss, num_rs, sci_ss, sci_rs, red_ss, red_rs,
):
    region = lax.axis_index("region")
    dev = lax.axis_index("dev")
    x = dev // RES
    r = dev % RES
    y = r // 2
    z = r % 2
    total_devs = regions * RES * NX
    whole = region * (RES * NX) + dev

    def order(i):
        return (3 * i) % RES

    def peer(t):
        return ((y + t // 2) % 4) * 2 + (z + t % 2) % 2

    def giver(t):
        return ((y + 4 - t // 2) % 4) * 2 + (z + t % 2) % 2

    def plane_id(res):
        return {"dev": x * RES + res}

    def line_id(dx):
        return {"dev": ((x + dx) % NX) * RES + r}

    def sky_id(step):
        other = (whole + step + total_devs) % total_devs
        return {"region": other // (RES * NX), "dev": other % (RES * NX)}

    def sci_copy(h, t, slot):
        return pltpu.make_async_remote_copy(
            src_ref=pack.at[h, t], dst_ref=recv.at[h, slot],
            send_sem=sci_ss.at[h, t], recv_sem=sci_rs.at[h, slot],
            device_id=plane_id(peer(t)), device_id_type=MESH)

    def tab_copy(t, slot):
        return pltpu.make_async_remote_copy(
            src_ref=tab, dst_ref=tabs.at[slot],
            send_sem=tab_ss.at[t], recv_sem=tab_rs.at[slot],
            device_id=plane_id(peer(t)), device_id_type=MESH)

    def num_copy(t, slot):
        return pltpu.make_async_remote_copy(
            src_ref=num, dst_ref=nums.at[slot],
            send_sem=num_ss.at[t], recv_sem=num_rs.at[slot],
            device_id=plane_id(peer(t)), device_id_type=MESH)

    def sky_copy(dx, slot):
        return pltpu.make_async_remote_copy(
            src_ref=sky.at[x], dst_ref=sky.at[slot],
            send_sem=sky_ss.at[dx], recv_sem=sky_rs.at[slot],
            device_id=line_id(dx), device_id_type=MESH)

    def fwd_copy(dx, slot):
        return pltpu.make_async_remote_copy(
            src_ref=edge.at[x], dst_ref=edge.at[slot],
            send_sem=fwd_ss.at[dx], recv_sem=fwd_rs.at[slot],
            device_id=line_id(dx), device_id_type=MESH)

    def edge_copy(side):
        rows = pl.ds(2 * (BLK - EDGE), 2 * EDGE) if side == 0 else pl.ds(0, 2 * EDGE)
        return pltpu.make_async_remote_copy(
            src_ref=sky.at[x, rows], dst_ref=edge.at[x_of(side), side],
            send_sem=edge_ss.at[side], recv_sem=edge_rs.at[side],
            device_id=sky_id(1 if side == 0 else -1), device_id_type=MESH)

    def x_of(side):
        other = (whole + (1 if side == 0 else -1) + total_devs) % total_devs
        return (other % (RES * NX)) // RES

    def edge_arrival(side):
        rows = pl.ds(2 * (BLK - EDGE), 2 * EDGE) if side == 0 else pl.ds(0, 2 * EDGE)
        return pltpu.make_async_remote_copy(
            src_ref=sky.at[x, rows], dst_ref=edge.at[x, side],
            send_sem=edge_ss.at[side], recv_sem=edge_rs.at[side],
            device_id=sky_id(1 if side == 0 else -1), device_id_type=MESH)

    def red_copy(h, dx, slot):
        return pltpu.make_async_remote_copy(
            src_ref=acc.at[h, (x + dx) % NX], dst_ref=part.at[h, slot],
            send_sem=red_ss.at[h, dx], recv_sem=red_rs.at[h, slot],
            device_id=line_id(dx), device_id_type=MESH)

    start_load = pltpu.make_async_copy(start_hbm, start_ref, loc_sem.at[6])
    start_load.start()
    coef_load = pltpu.make_async_copy(coef_hbm, coef_ref, loc_sem.at[7])
    coef_load.start()
    norm_load = pltpu.make_async_copy(norm_hbm, norm_ref, loc_sem.at[8])
    norm_load.start()
    sky_load = pltpu.make_async_copy(sky_hbm, sky.at[x], loc_sem.at[0])
    sky_load.start()
    sci = (sci0, sci1, sci2, sci3)
    sci_load = [pltpu.make_async_copy(sci_hbm.at[:, :, q], sci[q], loc_sem.at[9 + q]) for q in range(NQ)]
    for load in sci_load:
        load.start()
    across_load = pltpu.make_async_copy(across_hbm, across, loc_sem.at[2])
    across_load.start()
    down_load = pltpu.make_async_copy(down_hbm, down, loc_sem.at[3])
    down_load.start()

    barrier = pltpu.get_barrier_semaphore()

    def greet(t, carry):
        pl.semaphore_signal(barrier, inc=1, device_id=plane_id(peer(t)), device_id_type=MESH)
        return carry

    lax.fori_loop(1, RES, greet, 0)
    for dx in range(1, NX):
        pl.semaphore_signal(barrier, inc=1, device_id=line_id(dx), device_id_type=MESH)
    for step in (1, -1):
        pl.semaphore_signal(barrier, inc=1, device_id=sky_id(step), device_id_type=MESH)

    lanes = lax.broadcasted_iota(jnp.int32, (8, CW), 1)
    acc[...] = jnp.zeros(acc.shape, F32)
    for block in range(NX):
        for profile in range(NPROF):
            wide[block, profile, 3 * EXT : DEPTH, :] = jnp.zeros((DEPTH - 3 * EXT, CW), BF16)

    start_load.wait()
    coef_load.wait()
    norm_load.wait()
    tab[...] = jnp.zeros((8, CW), F32)
    for term in range(3):
        tab[2 * term : 2 * term + 2, 0:NBASIS] = coef_ref[term]
    raw = tab[...]
    weighted = jnp.sum(raw * norm_ref[...], axis=1, keepdims=True)
    tab[...] = jnp.where(lanes == NBASIS, weighted, raw)
    starts = (start_ref[0, 0], start_ref[0, 1])
    num[...] = jnp.where(lanes == 0, starts[0], starts[1])
    tabs[r] = tab[...]
    nums[r] = num[...]

    sky_load.wait()
    pl.semaphore_wait(barrier, RES - 1 + NX - 1 + 2)

    for side in (0, 1):
        edge_copy(side).start()
    for dx in range(1, NX):
        sky_copy(dx, x).start()

    def chosen(q, res, e):
        block = lax.rem(res - starts[e] + 4 * RES, RES)
        return sci[q][e, block]

    for q in range(NQ):
        sci_load[q].wait()

        def give(i, carry):
            t = order(i)
            for e in range(2):
                pack[q, t, e] = chosen(q, peer(t), e)
            sci_copy(q, t, r).start()
            return carry

        lax.fori_loop(1, RES, give, 0)
        for e in range(2):
            recv[q, r, e] = chosen(q, r, e)
        if q == 0:
            def give_tables(i, carry):
                t = order(i)
                tab_copy(t, r).start()
                num_copy(t, r).start()
                return carry

            lax.fori_loop(1, RES, give_tables, 0)
        if q == 1:
            for side in (0, 1):
                edge_arrival(side).wait_recv()
            for dx in range(1, NX):
                fwd_copy(dx, x).start()

    across_load.wait()

    def spread_across(rows, places):
        high = rows.astype(BF16)
        rest = (rows - high.astype(F32)).astype(BF16)
        lhs = jnp.concatenate([high, rest, high], axis=1)
        for tile in range(NPROF // 2):
            both = jnp.dot(lhs, across[tile], preferred_element_type=F32)
            for side in range(2):
                values = both[:, side * CW : (side + 1) * CW]
                high = values.astype(BF16)
                rest = (values - high.astype(F32)).astype(BF16)
                profile = 2 * tile + side
                for block, first, count, to in places:
                    wide[block, profile, to : to + count, :] = high[first : first + count]
                    wide[block, profile, EXT + to : EXT + to + count, :] = high[first : first + count]
                    wide[block, profile, 2 * EXT + to : 2 * EXT + to + count, :] = rest[first : first + count]

    def body_rows(block):
        for q in range(NQ):
            skyvar[block, q] = sky[block, pl.ds(q * 2 * PART + 1, PART, stride=2), :]
        return sky[block, pl.ds(0, BLK, stride=2), :]

    def smooth(pair):
        for across_profile in range(NPROF):
            users = [(k, v) for k, (v, a) in enumerate(BASIS) if a == across_profile]
            low_v = users[0][1]
            result = jnp.dot(
                down[low_v * BLK : (low_v + len(users)) * BLK, :],
                jnp.concatenate([wide[2 * pair, across_profile], wide[2 * pair + 1, across_profile]], axis=1),
                preferred_element_type=F32)
            for place, (k, v) in enumerate(users):
                for side in range(2):
                    for q in range(NQ):
                        row = place * BLK + q * PART
                        basis[2 * pair + side, k, q] = result[row : row + PART, side * CW : (side + 1) * CW]

    near = 2 * (x // 2) + 1 - x % 2
    far = 2 * (1 - x // 2)
    spread_across(body_rows(x), [(x, 0, BLK, 0)])
    sky_copy(1, near).wait_recv()
    spread_across(body_rows(near), [(near, 0, BLK, 0)])

    sky_top = (region == 0) & (r == 0)
    sky_end = (region == regions - 1) & (r == RES - 1)
    fwd_copy(1, near).wait_recv()
    for side in range(2):
        fwd_copy(1, far + side).wait_recv()
    rims = []
    for block in range(NX):
        top = edge[block, 0, pl.ds(0, EDGE, stride=2), :]
        low = edge[block, 1, pl.ds(0, EDGE, stride=2), :]
        if block == 0:
            top = jnp.where(sky_top, 0.0, top)
        if block == NX - 1:
            low = jnp.where(sky_end, 0.0, low)
        rims += [low, top]
    spread_across(
        jnp.concatenate(rims, axis=0), [(block, 2 * EDGE * block, 2 * EDGE, BLK) for block in range(NX)])
    down_load.wait()
    smooth(x // 2)
    for side in range(2):
        sky_copy(1, far + side).wait_recv()
    spread_across(
        jnp.concatenate([body_rows(far), body_rows(far + 1)], axis=0),
        [(far, 0, BLK, 0), (far + 1, BLK, BLK, 0)])
    smooth(1 - x // 2)

    def tables(t, carry):
        tab_copy(t, giver(t)).wait_recv()
        num_copy(t, giver(t)).wait_recv()
        return carry

    lax.fori_loop(1, RES, tables, 0)
    tab_move = pltpu.make_async_copy(tabs, tab_s, loc_sem.at[4])
    tab_move.start()
    num_move = pltpu.make_async_copy(nums, num_s, loc_sem.at[5])
    num_move.start()
    tab_move.wait()
    num_move.wait()

    xs = (2.0 * lanes.astype(F32) + 1.0) / CW - 1.0
    rows = (8 * lax.broadcasted_iota(jnp.int32, (TILES, 8, CW), 0)
            + lax.broadcasted_iota(jnp.int32, (TILES, 8, CW), 1)).astype(F32)
    ys_base = (2.0 * rows + 1.0) / (RES * BLK)

    def work(q, t):
        source = giver(t)
        found = []
        for e in range(2):
            start = num_s[source, 0, e]
            place = lax.rem(r - start + 4 * RES, RES)
            block = (start + place) // RES
            flat = jnp.zeros((TILES, 8, CW), F32)
            slope = jnp.zeros((TILES, 8, CW), F32)
            for k in range(NBASIS):
                image = basis[block, k, q].reshape(TILES, 8, CW)
                factor = tab_s[source, e, k] + tab_s[source, 2 + e, k] * xs
                flat = flat + factor[None] * image
                slope = slope + tab_s[source, 4 + e, k] * image
            y0 = (place * BLK + q * PART).astype(F32)
            ys = ys_base + (y0 * (2.0 / (RES * BLK)) - 1.0)
            gain = (tab_s[source, e, NBASIS] + tab_s[source, 2 + e, NBASIS] * xs)[None] + tab_s[
                source, 4 + e, NBASIS] * ys
            flux = recv[q, source, e, pl.ds(0, PART, stride=2), :].reshape(TILES, 8, CW)
            noise = recv[q, source, e, pl.ds(1, PART, stride=2), :].reshape(TILES, 8, CW)
            behind = skyvar[block, q].reshape(TILES, 8, CW)
            weight = 1.0 / (noise + gain * gain * behind)
            diff = (flux - (flat + ys * slope)) * weight
            found.append((block, diff.reshape(PART, CW), weight.reshape(PART, CW)))
        for target in range(NX):
            for plane in range(2):
                span = slice(plane * PART, (plane + 1) * PART)
                old = acc[q, target, span, :]
                for block, diff, weight in found:
                    old = old + jnp.where(block == target, weight if plane else diff, 0.0)
                acc[q, target, span, :] = old

    def finish(q):
        for dx in range(1, NX):
            red_copy(q, dx, (x + dx) % NX).wait_recv()
        total = acc[q, x]
        for dx in range(1, NX):
            total = total + part[q, (x + dx) % NX]
        for plane in range(2):
            out_ref[pl.ds(q * 2 * PART + plane, PART, stride=2), :] = total[plane * PART : (plane + 1) * PART]

    for q in range(NQ):
        work(q, 0)

        def take(i, carry):
            t = order(i)
            sci_copy(q, t, giver(t)).wait_recv()
            work(q, t)
            return carry

        lax.fori_loop(1, RES, take, 0)
        for dx in range(1, NX):
            red_copy(q, dx, x).start()
        if q > 0:
            finish(q - 1)
    finish(NQ - 1)

    for side in (0, 1):
        edge_copy(side).wait_send()
    for dx in range(1, NX):
        sky_copy(dx, x).wait_send()
        fwd_copy(dx, x).wait_send()
        for q in range(NQ):
            red_copy(q, dx, x).wait_send()

    def sent(t, carry):
        tab_copy(t, r).wait_send()
        num_copy(t, r).wait_send()
        for q in range(NQ):
            sci_copy(q, t, r).wait_send()
        return carry

    lax.fori_loop(1, RES, sent, 0)


def per_device(science, coadd, coefficients, strip_start):
    regions = lax.axis_size("region")
    across_np, down_np, norms_np = constant_matrices()
    sci = science.reshape(2, RES, NQ, 2 * PART, CW)
    sky = coadd.reshape(2 * BLK, CW)
    coef = jnp.transpose(coefficients[0, 0], (2, 0, 1))
    starts = strip_start[0]
    dma = pltpu.SemaphoreType.DMA
    scratch = [
        *[pltpu.VMEM((2, RES, 2 * PART, CW), F32) for q in range(NQ)],
        pltpu.VMEM((NQ, RES, 2, 2 * PART, CW), F32),
        pltpu.VMEM((NQ, RES, 2, 2 * PART, CW), F32),
        pltpu.VMEM((NX, 2 * BLK, CW), F32),
        pltpu.VMEM((NX, 2, 2 * EDGE, CW), F32),
        pltpu.VMEM(across_np.shape, BF16),
        pltpu.VMEM(down_np.shape, BF16),
        pltpu.VMEM((NX, NPROF, DEPTH, CW), BF16),
        pltpu.VMEM((NX, NBASIS, NQ, PART, CW), F32),
        pltpu.VMEM((NX, NQ, PART, CW), F32),
        pltpu.VMEM((NQ, NX, 2 * PART, CW), F32),
        pltpu.VMEM((NQ, NX, 2 * PART, CW), F32),
        pltpu.VMEM((8, CW), F32),
        pltpu.VMEM((RES, 8, CW), F32),
        pltpu.VMEM((8, CW), jnp.int32),
        pltpu.VMEM((RES, 8, CW), jnp.int32),
        pltpu.SMEM((RES, 8, CW), F32),
        pltpu.SMEM((RES, 8, CW), jnp.int32),
        pltpu.VMEM((3, 2, NBASIS), F32),
        pltpu.SMEM((1, 2), jnp.int32),
        pltpu.VMEM((8, CW), F32),
        dma((9 + NQ,)),
        dma((NX,)), dma((NX,)),
        dma((2,)), dma((2,)),
        dma((NX,)), dma((NX,)),
        dma((RES,)), dma((RES,)),
        dma((RES,)), dma((RES,)),
        dma((NQ, RES)), dma((NQ, RES)),
        dma((NQ, NX)), dma((NQ, NX)),
    ]
    hbm = pl.BlockSpec(memory_space=pl.ANY)
    vmem = pl.BlockSpec(memory_space=pltpu.VMEM)
    result = pl.pallas_call(
        lambda *refs: kernel(regions, *refs),
        out_shape=jax.ShapeDtypeStruct((2 * BLK, CW), F32),
        in_specs=[hbm] * 7,
        out_specs=vmem,
        scratch_shapes=scratch,
        compiler_params=pltpu.CompilerParams(
            collective_id=0, has_side_effects=True, vmem_limit_bytes=62 * 1024 * 1024),
        cost_estimate=pl.CostEstimate(flops=3_000_000_000, bytes_accessed=6_000_000, transcendentals=0),
        name="difference_sums",
    )(sci, sky, coef, starts, jnp.asarray(across_np), jnp.asarray(down_np), jnp.asarray(norms_np))
    return result.reshape(1, BLK, 2, CW)


def solution(mesh):
    placed = (
        P("region", "dev", None, None, None, None),
        P("region", "dev", None, None),
        P("region", "dev", None, None, None),
        P("region", "dev", None),
    )
    return jax.shard_map(
        per_device,
        mesh=mesh,
        in_specs=placed,
        out_specs=P("region", "dev", None, None),
        check_vma=False,
    )
```

time: 46.5 us -> 40.2 us (0.86)
  the two profiles are of different devices: /device:TPU:0 before, /device:TPU:32 now
where the time goes in v2:
time: 40.2 us; the launch traced here: 40.1 us
  Pallas kernels  38.5 us (96%)
  local copies, waits for them, and re-layouts  1.57 us (4%)
    pallas_call x1, Pallas kernels, per_device(): pl.pallas_call(lambda *refs: kernel(regions, *refs), out_shape=jax.ShapeD...  38.5 us
    unnamed x1, local copies, waits for them, and re-layouts  1.57 us

profile of v2, /device:TPU:32, one launch (start us, length us, event | category | flops | bytes accessed | tf_op | source)
XLA Modules:
  0.0 40.1 jit_solution(4209443094747106025)
XLA Ops:
  0.0 38.5 %difference_sums.1 = f32[256,128]{1,0:T(8,128)} custom-call(f32[2,8,4,64,128]{4,3,2,1,0:T(8,128)} %bitcast.8, f32[256,128]{1,0:T(8,128)} %bitcast.9, f32[3,2,31]{2,1,0:T(2,128)} %bitcast.10, s32[1,2]{1,0:T(1,128)} %bitcast.11, bf16[6,384,256]{2,1,0:T(8,128)(2,1)} %constant.6.clone.refs_4_, bf16[1536,512]{1,0:T(8,128)(2,1)} %constant.7.clone.refs_5_, ...), custom_call_target="tpu_custom_call" | custom-call | flops 3000000000 | bytes 6000000 | tf_op jit(solution)/shard_map/difference_sums/pallas_call | solution.py:468
  38.5 1.6 %copy.9 = f32[1,128,2,128]{3,2,1,0:T(2,128)} copy(f32[1,128,2,128]{3,2,1,0:T(2,128)} %bitcast.7) | data formatting | bytes 262144

commit v3 on v2

--- a/solution.py
+++ b/solution.py
@@ -20,9 +20,9 @@
 EDGE = 16
 EXT = BLK + 2 * EDGE
 DEPTH = 512
-NQ = 4
-PART = BLK // NQ
-TILES = PART // 8
+CHUNKS = (32, 32, 32, 32)
+NQ = len(CHUNKS)
+FIRST = tuple(sum(CHUNKS[:q]) for q in range(NQ))
 F32 = jnp.float32
 BF16 = jnp.bfloat16
 MESH = pl.DeviceIdType.MESH
@@ -88,8 +88,8 @@
     regions,
     sci_hbm, sky_hbm, coef_hbm, start_hbm, across_hbm, down_hbm, norm_hbm,
     out_ref,
-    sci0, sci1, sci2, sci3, pack, recv, sky, edge, across, down, wide, basis, skyvar,
-    acc, part, tab, tabs, num, nums, tab_s, num_s, coef_ref, start_ref, norm_ref,
+    sci, pack, recv, basis, skyvar, acc, part,
+    sky, edge, across, down, wide, tab, tabs, num, nums, tab_s, num_s, coef_ref, start_ref, norm_ref,
     loc_sem, sky_ss, sky_rs, edge_ss, edge_rs, fwd_ss, fwd_rs,
     tab_ss, tab_rs, num_ss, num_rs, sci_ss, sci_rs, red_ss, red_rs,
 ):
@@ -123,7 +123,7 @@
 
     def sci_copy(h, t, slot):
         return pltpu.make_async_remote_copy(
-            src_ref=pack.at[h, t], dst_ref=recv.at[h, slot],
+            src_ref=pack[h].at[t], dst_ref=recv[h].at[slot],
             send_sem=sci_ss.at[h, t], recv_sem=sci_rs.at[h, slot],
             device_id=plane_id(peer(t)), device_id_type=MESH)
 
@@ -171,26 +171,24 @@
 
     def red_copy(h, dx, slot):
         return pltpu.make_async_remote_copy(
-            src_ref=acc.at[h, (x + dx) % NX], dst_ref=part.at[h, slot],
+            src_ref=acc[h].at[(x + dx) % NX], dst_ref=part[h].at[slot],
             send_sem=red_ss.at[h, dx], recv_sem=red_rs.at[h, slot],
             device_id=line_id(dx), device_id_type=MESH)
 
-    start_load = pltpu.make_async_copy(start_hbm, start_ref, loc_sem.at[6])
-    start_load.start()
-    coef_load = pltpu.make_async_copy(coef_hbm, coef_ref, loc_sem.at[7])
-    coef_load.start()
-    norm_load = pltpu.make_async_copy(norm_hbm, norm_ref, loc_sem.at[8])
-    norm_load.start()
-    sky_load = pltpu.make_async_copy(sky_hbm, sky.at[x], loc_sem.at[0])
-    sky_load.start()
-    sci = (sci0, sci1, sci2, sci3)
-    sci_load = [pltpu.make_async_copy(sci_hbm.at[:, :, q], sci[q], loc_sem.at[9 + q]) for q in range(NQ)]
-    for load in sci_load:
-        load.start()
-    across_load = pltpu.make_async_copy(across_hbm, across, loc_sem.at[2])
-    across_load.start()
-    down_load = pltpu.make_async_copy(down_hbm, down, loc_sem.at[3])
-    down_load.start()
+    def load(source, target, number):
+        copy = pltpu.make_async_copy(source, target, loc_sem.at[number])
+        copy.start()
+        return copy
+
+    def load_science(q):
+        rows = pl.ds(2 * FIRST[q], 2 * CHUNKS[q])
+        return load(sci_hbm.at[:, :, rows], sci[q], 9 + q)
+
+    start_load = load(start_hbm, start_ref, 6)
+    sky_load = load(sky_hbm, sky.at[x], 0)
+    coef_load = load(coef_hbm, coef_ref, 7)
+    norm_load = load(norm_hbm, norm_ref, 8)
+    sci_load = [load_science(0)]
 
     barrier = pltpu.get_barrier_semaphore()
 
@@ -204,13 +202,14 @@
     for step in (1, -1):
         pl.semaphore_signal(barrier, inc=1, device_id=sky_id(step), device_id_type=MESH)
 
+    sci_load += [load_science(q) for q in range(1, NQ)]
+    across_load = load(across_hbm, across, 2)
+    down_load = load(down_hbm, down, 3)
+
     lanes = lax.broadcasted_iota(jnp.int32, (8, CW), 1)
-    acc[...] = jnp.zeros(acc.shape, F32)
-    for block in range(NX):
-        for profile in range(NPROF):
-            wide[block, profile, 3 * EXT : DEPTH, :] = jnp.zeros((DEPTH - 3 * EXT, CW), BF16)
-
     start_load.wait()
+    starts = (start_ref[0, 0], start_ref[0, 1])
+    num[...] = jnp.where(lanes[0:1] == 0, starts[0], starts[1])
     coef_load.wait()
     norm_load.wait()
     tab[...] = jnp.zeros((8, CW), F32)
@@ -219,8 +218,6 @@
     raw = tab[...]
     weighted = jnp.sum(raw * norm_ref[...], axis=1, keepdims=True)
     tab[...] = jnp.where(lanes == NBASIS, weighted, raw)
-    starts = (start_ref[0, 0], start_ref[0, 1])
-    num[...] = jnp.where(lanes == 0, starts[0], starts[1])
     tabs[r] = tab[...]
     nums[r] = num[...]
 
@@ -242,13 +239,13 @@
         def give(i, carry):
             t = order(i)
             for e in range(2):
-                pack[q, t, e] = chosen(q, peer(t), e)
+                pack[q][t, e] = chosen(q, peer(t), e)
             sci_copy(q, t, r).start()
             return carry
 
         lax.fori_loop(1, RES, give, 0)
         for e in range(2):
-            recv[q, r, e] = chosen(q, r, e)
+            recv[q][r, e] = chosen(q, r, e)
         if q == 0:
             def give_tables(i, carry):
                 t = order(i)
@@ -263,6 +260,11 @@
             for dx in range(1, NX):
                 fwd_copy(dx, x).start()
 
+    for q in range(NQ):
+        acc[q][...] = jnp.zeros(acc[q].shape, F32)
+    for block in range(NX):
+        for profile in range(NPROF):
+            wide[block, profile, 3 * EXT : DEPTH, :] = jnp.zeros((DEPTH - 3 * EXT, CW), BF16)
     across_load.wait()
 
     def spread_across(rows, places):
@@ -283,7 +285,7 @@
 
     def body_rows(block):
         for q in range(NQ):
-            skyvar[block, q] = sky[block, pl.ds(q * 2 * PART + 1, PART, stride=2), :]
+            skyvar[q][block] = sky[block, pl.ds(2 * FIRST[q] + 1, CHUNKS[q], stride=2), :]
         return sky[block, pl.ds(0, BLK, stride=2), :]
 
     def smooth(pair):
@@ -297,8 +299,8 @@
             for place, (k, v) in enumerate(users):
                 for side in range(2):
                     for q in range(NQ):
-                        row = place * BLK + q * PART
-                        basis[2 * pair + side, k, q] = result[row : row + PART, side * CW : (side + 1) * CW]
+                        row = place * BLK + FIRST[q]
+                        basis[q][2 * pair + side, k] = result[row : row + CHUNKS[q], side * CW : (side + 1) * CW]
 
     near = 2 * (x // 2) + 1 - x % 2
     far = 2 * (1 - x // 2)
@@ -345,50 +347,52 @@
     num_move.wait()
 
     xs = (2.0 * lanes.astype(F32) + 1.0) / CW - 1.0
-    rows = (8 * lax.broadcasted_iota(jnp.int32, (TILES, 8, CW), 0)
-            + lax.broadcasted_iota(jnp.int32, (TILES, 8, CW), 1)).astype(F32)
-    ys_base = (2.0 * rows + 1.0) / (RES * BLK)
 
     def work(q, t):
         source = giver(t)
+        count = CHUNKS[q]
+        shape = (count // 8, 8, CW)
+        rows = (8 * lax.broadcasted_iota(jnp.int32, shape, 0) + lax.broadcasted_iota(jnp.int32, shape, 1)).astype(F32)
+        ys_base = (2.0 * rows + 1.0) / (RES * BLK)
         found = []
         for e in range(2):
             start = num_s[source, 0, e]
             place = lax.rem(r - start + 4 * RES, RES)
             block = (start + place) // RES
-            flat = jnp.zeros((TILES, 8, CW), F32)
-            slope = jnp.zeros((TILES, 8, CW), F32)
+            flat = jnp.zeros(shape, F32)
+            slope = jnp.zeros(shape, F32)
             for k in range(NBASIS):
-                image = basis[block, k, q].reshape(TILES, 8, CW)
+                image = basis[q][block, k].reshape(shape)
                 factor = tab_s[source, e, k] + tab_s[source, 2 + e, k] * xs
                 flat = flat + factor[None] * image
                 slope = slope + tab_s[source, 4 + e, k] * image
-            y0 = (place * BLK + q * PART).astype(F32)
+            y0 = (place * BLK + FIRST[q]).astype(F32)
             ys = ys_base + (y0 * (2.0 / (RES * BLK)) - 1.0)
             gain = (tab_s[source, e, NBASIS] + tab_s[source, 2 + e, NBASIS] * xs)[None] + tab_s[
                 source, 4 + e, NBASIS] * ys
-            flux = recv[q, source, e, pl.ds(0, PART, stride=2), :].reshape(TILES, 8, CW)
-            noise = recv[q, source, e, pl.ds(1, PART, stride=2), :].reshape(TILES, 8, CW)
-            behind = skyvar[block, q].reshape(TILES, 8, CW)
+            flux = recv[q][source, e, pl.ds(0, count, stride=2), :].reshape(shape)
+            noise = recv[q][source, e, pl.ds(1, count, stride=2), :].reshape(shape)
+            behind = skyvar[q][block].reshape(shape)
             weight = 1.0 / (noise + gain * gain * behind)
             diff = (flux - (flat + ys * slope)) * weight
-            found.append((block, diff.reshape(PART, CW), weight.reshape(PART, CW)))
+            found.append((block, diff.reshape(count, CW), weight.reshape(count, CW)))
         for target in range(NX):
             for plane in range(2):
-                span = slice(plane * PART, (plane + 1) * PART)
-                old = acc[q, target, span, :]
+                span = slice(plane * count, (plane + 1) * count)
+                old = acc[q][target, span, :]
                 for block, diff, weight in found:
                     old = old + jnp.where(block == target, weight if plane else diff, 0.0)
-                acc[q, target, span, :] = old
+                acc[q][target, span, :] = old
 
     def finish(q):
         for dx in range(1, NX):
             red_copy(q, dx, (x + dx) % NX).wait_recv()
-        total = acc[q, x]
+        count = CHUNKS[q]
+        total = acc[q][x]
         for dx in range(1, NX):
-            total = total + part[q, (x + dx) % NX]
+            total = total + part[q][(x + dx) % NX]
         for plane in range(2):
-            out_ref[pl.ds(q * 2 * PART + plane, PART, stride=2), :] = total[plane * PART : (plane + 1) * PART]
+            out_ref[pl.ds(2 * FIRST[q] + plane, count, stride=2), :] = total[plane * count : (plane + 1) * count]
 
     for q in range(NQ):
         work(q, 0)
@@ -427,30 +431,32 @@
 def per_device(science, coadd, coefficients, strip_start):
     regions = lax.axis_size("region")
     across_np, down_np, norms_np = constant_matrices()
-    sci = science.reshape(2, RES, NQ, 2 * PART, CW)
+    sci = science.reshape(2, RES, 2 * BLK, CW)
     sky = coadd.reshape(2 * BLK, CW)
     coef = jnp.transpose(coefficients[0, 0], (2, 0, 1))
     starts = strip_start[0]
     dma = pltpu.SemaphoreType.DMA
+    def chunked(*lead):
+        return [pltpu.VMEM((*lead, 2 * count, CW), F32) for count in CHUNKS]
+
+    def single(*lead):
+        return [pltpu.VMEM((*lead, count, CW), F32) for count in CHUNKS]
+
     scratch = [
-        *[pltpu.VMEM((2, RES, 2 * PART, CW), F32) for q in range(NQ)],
-        pltpu.VMEM((NQ, RES, 2, 2 * PART, CW), F32),
-        pltpu.VMEM((NQ, RES, 2, 2 * PART, CW), F32),
+        chunked(2, RES), chunked(RES, 2), chunked(RES, 2),
+        single(NX, NBASIS), single(NX),
+        chunked(NX), chunked(NX),
         pltpu.VMEM((NX, 2 * BLK, CW), F32),
         pltpu.VMEM((NX, 2, 2 * EDGE, CW), F32),
         pltpu.VMEM(across_np.shape, BF16),
         pltpu.VMEM(down_np.shape, BF16),
         pltpu.VMEM((NX, NPROF, DEPTH, CW), BF16),
-        pltpu.VMEM((NX, NBASIS, NQ, PART, CW), F32),
-        pltpu.VMEM((NX, NQ, PART, CW), F32),
-        pltpu.VMEM((NQ, NX, 2 * PART, CW), F32),
-        pltpu.VMEM((NQ, NX, 2 * PART, CW), F32),
         pltpu.VMEM((8, CW), F32),
         pltpu.VMEM((RES, 8, CW), F32),
-        pltpu.VMEM((8, CW), jnp.int32),
-        pltpu.VMEM((RES, 8, CW), jnp.int32),
+        pltpu.VMEM((1, CW), jnp.int32),
+        pltpu.VMEM((RES, 1, CW), jnp.int32),
         pltpu.SMEM((RES, 8, CW), F32),
-        pltpu.SMEM((RES, 8, CW), jnp.int32),
+        pltpu.SMEM((RES, 1, CW), jnp.int32),
         pltpu.VMEM((3, 2, NBASIS), F32),
         pltpu.SMEM((1, 2), jnp.int32),
         pltpu.VMEM((8, CW), F32),
@@ -463,6 +469,7 @@
         dma((NQ, RES)), dma((NQ, RES)),
         dma((NQ, NX)), dma((NQ, NX)),
     ]
+    operands = (sci, sky, coef, starts, jnp.asarray(across_np), jnp.asarray(down_np), jnp.asarray(norms_np))
     hbm = pl.BlockSpec(memory_space=pl.ANY)
     vmem = pl.BlockSpec(memory_space=pltpu.VMEM)
     result = pl.pallas_call(
@@ -472,10 +479,10 @@
         out_specs=vmem,
         scratch_shapes=scratch,
         compiler_params=pltpu.CompilerParams(
-            collective_id=0, has_side_effects=True, vmem_limit_bytes=62 * 1024 * 1024),
+            collective_id=0, has_side_effects=True, vmem_limit_bytes=52 * 1024 * 1024),
         cost_estimate=pl.CostEstimate(flops=3_000_000_000, bytes_accessed=6_000_000, transcendentals=0),
         name="difference_sums",
-    )(sci, sky, coef, starts, jnp.asarray(across_np), jnp.asarray(down_np), jnp.asarray(norms_np))
+    )(*[pltpu.with_memory_space_constraint(operand, pltpu.HBM) for operand in operands])
     return result.reshape(1, BLK, 2, CW)
 
 

time: 40.2 us -> 38.2 us (0.950)
  Pallas kernels: 38.5 us -> 37.4 us
  local copies, waits for them, and re-layouts: 1.57 us -> 0.66 us
    pallas_call x1, Pallas kernels: 38.5 us -> 37.4 us  [per_device(): pl.pallas_call(lambda *refs: kernel(regions, *refs), out_shape=jax.ShapeD...]
    unnamed x1, local copies, waits for them, and re-layouts: 1.57 us -> 0.66 us
where the time goes in v3:
time: 38.2 us; the launch traced here: 38.1 us
  Pallas kernels  37.4 us (98%)
  local copies, waits for them, and re-layouts  0.66 us (2%)
    pallas_call x1, Pallas kernels, per_device(): pl.pallas_call(lambda *refs: kernel(regions, *refs), out_shape=jax.ShapeD...  37.4 us

profile of v3, /device:TPU:32, one launch (start us, length us, event | category | flops | bytes accessed | tf_op | source)
XLA Modules:
  0.0 38.1 jit_solution(10529787123725840355)
XLA Ops:
  0.0 37.4 %difference_sums.1 = f32[256,128]{1,0:T(8,128)S(1)} custom-call(f32[2,8,256,128]{3,2,1,0:T(8,128)} %bitcast.8, f32[256,128]{1,0:T(8,128)} %bitcast.9, f32[3,2,31]{2,1,0:T(2,128)} %bitcast.10, s32[1,2]{1,0:T(1,128)} %bitcast.11, bf16[6,384,256]{2,1,0:T(8,128)(2,1)} %constant.6.clone.refs_4_, bf16[1536,512]{1,0:T(8,128)(2,1)} %constant.7.clone.refs_5_, ...), custom_call_target="tpu_custom_call" | custom-call | flops 3000000000 | bytes 6000000 | tf_op jit(solution)/shard_map/difference_sums/pallas_call | solution.py:475
  37.4 0.7 %copy.9 = f32[1,128,2,128]{3,2,1,0:T(2,128)} copy(f32[1,128,2,128]{3,2,1,0:T(2,128)S(1)} %bitcast.7) | data formatting | bytes 262144

commit v4 on v3

--- a/solution.py
+++ b/solution.py
@@ -20,7 +20,7 @@
 EDGE = 16
 EXT = BLK + 2 * EDGE
 DEPTH = 512
-CHUNKS = (32, 32, 32, 32)
+CHUNKS = (16, 40, 56, 16)
 NQ = len(CHUNKS)
 FIRST = tuple(sum(CHUNKS[:q]) for q in range(NQ))
 F32 = jnp.float32
@@ -88,7 +88,7 @@
     regions,
     sci_hbm, sky_hbm, coef_hbm, start_hbm, across_hbm, down_hbm, norm_hbm,
     out_ref,
-    sci, pack, recv, basis, skyvar, acc, part,
+    sci, pack, recv, basis, skyvar, modelled, acc, part,
     sky, edge, across, down, wide, tab, tabs, num, nums, tab_s, num_s, coef_ref, start_ref, norm_ref,
     loc_sem, sky_ss, sky_rs, edge_ss, edge_rs, fwd_ss, fwd_rs,
     tab_ss, tab_rs, num_ss, num_rs, sci_ss, sci_rs, red_ss, red_rs,
@@ -348,13 +348,11 @@
 
     xs = (2.0 * lanes.astype(F32) + 1.0) / CW - 1.0
 
-    def work(q, t):
+    def model(q, t):
         source = giver(t)
-        count = CHUNKS[q]
-        shape = (count // 8, 8, CW)
+        shape = (CHUNKS[q] // 8, 8, CW)
         rows = (8 * lax.broadcasted_iota(jnp.int32, shape, 0) + lax.broadcasted_iota(jnp.int32, shape, 1)).astype(F32)
         ys_base = (2.0 * rows + 1.0) / (RES * BLK)
-        found = []
         for e in range(2):
             start = num_s[source, 0, e]
             place = lax.rem(r - start + 4 * RES, RES)
@@ -370,12 +368,21 @@
             ys = ys_base + (y0 * (2.0 / (RES * BLK)) - 1.0)
             gain = (tab_s[source, e, NBASIS] + tab_s[source, 2 + e, NBASIS] * xs)[None] + tab_s[
                 source, 4 + e, NBASIS] * ys
-            flux = recv[q][source, e, pl.ds(0, count, stride=2), :].reshape(shape)
-            noise = recv[q][source, e, pl.ds(1, count, stride=2), :].reshape(shape)
             behind = skyvar[q][block].reshape(shape)
-            weight = 1.0 / (noise + gain * gain * behind)
-            diff = (flux - (flat + ys * slope)) * weight
-            found.append((block, diff.reshape(count, CW), weight.reshape(count, CW)))
+            modelled[q][source, e, 0] = (flat + ys * slope).reshape(CHUNKS[q], CW)
+            modelled[q][source, e, 1] = (gain * gain * behind).reshape(CHUNKS[q], CW)
+
+    def add(q, t):
+        source = giver(t)
+        count = CHUNKS[q]
+        found = []
+        for e in range(2):
+            start = num_s[source, 0, e]
+            block = (start + lax.rem(r - start + 4 * RES, RES)) // RES
+            flux = recv[q][source, e, pl.ds(0, count, stride=2), :]
+            noise = recv[q][source, e, pl.ds(1, count, stride=2), :]
+            weight = 1.0 / (noise + modelled[q][source, e, 1])
+            found.append((block, (flux - modelled[q][source, e, 0]) * weight, weight))
         for target in range(NX):
             for plane in range(2):
                 span = slice(plane * count, (plane + 1) * count)
@@ -395,12 +402,17 @@
             out_ref[pl.ds(2 * FIRST[q] + plane, count, stride=2), :] = total[plane * count : (plane + 1) * count]
 
     for q in range(NQ):
-        work(q, 0)
+        def prepare(t, carry):
+            model(q, t)
+            return carry
+
+        lax.fori_loop(0, RES, prepare, 0)
+        add(q, 0)
 
         def take(i, carry):
             t = order(i)
             sci_copy(q, t, giver(t)).wait_recv()
-            work(q, t)
+            add(q, t)
             return carry
 
         lax.fori_loop(1, RES, take, 0)
@@ -444,7 +456,7 @@
 
     scratch = [
         chunked(2, RES), chunked(RES, 2), chunked(RES, 2),
-        single(NX, NBASIS), single(NX),
+        single(NX, NBASIS), single(NX), single(RES, 2, 2),
         chunked(NX), chunked(NX),
         pltpu.VMEM((NX, 2 * BLK, CW), F32),
         pltpu.VMEM((NX, 2, 2 * EDGE, CW), F32),

time: 38.2 us -> 36.9 us (0.966)
  the two profiles are of different devices: /device:TPU:32 before, /device:TPU:0 now
where the time goes in v4:
time: 36.9 us; the launch traced here: 36.8 us
  Pallas kernels  36.2 us (98%)
  local copies, waits for them, and re-layouts  0.66 us (2%)
    pallas_call x1, Pallas kernels, per_device(): pl.pallas_call(lambda *refs: kernel(regions, *refs), out_shape=jax.ShapeD...  36.2 us

profile of v4, /device:TPU:0, one launch (start us, length us, event | category | flops | bytes accessed | tf_op | source)
XLA Modules:
  0.0 36.8 jit_solution(12251019173990032146)
XLA Ops:
  0.0 36.2 %difference_sums.1 = f32[256,128]{1,0:T(8,128)S(1)} custom-call(f32[2,8,256,128]{3,2,1,0:T(8,128)} %bitcast.8, f32[256,128]{1,0:T(8,128)} %bitcast.9, f32[3,2,31]{2,1,0:T(2,128)} %bitcast.10, s32[1,2]{1,0:T(1,128)} %bitcast.11, bf16[6,384,256]{2,1,0:T(8,128)(2,1)} %constant.6.clone.refs_4_, bf16[1536,512]{1,0:T(8,128)(2,1)} %constant.7.clone.refs_5_, ...), custom_call_target="tpu_custom_call" | custom-call | flops 3000000000 | bytes 6000000 | tf_op jit(solution)/shard_map/difference_sums/pallas_call | solution.py:487
  36.2 0.7 %copy.9 = f32[1,128,2,128]{3,2,1,0:T(2,128)} copy(f32[1,128,2,128]{3,2,1,0:T(2,128)S(1)} %bitcast.7) | data formatting | bytes 262144

commit v5 on v4

--- a/solution.py
+++ b/solution.py
@@ -20,7 +20,7 @@
 EDGE = 16
 EXT = BLK + 2 * EDGE
 DEPTH = 512
-CHUNKS = (16, 40, 56, 16)
+CHUNKS = (16, 48, 48, 16)
 NQ = len(CHUNKS)
 FIRST = tuple(sum(CHUNKS[:q]) for q in range(NQ))
 F32 = jnp.float32
@@ -103,7 +103,7 @@
     whole = region * (RES * NX) + dev
 
     def order(i):
-        return (3 * i) % RES
+        return (lax.shift_right_logical(jnp.int32(15394568), jnp.int32(3 * i)) % RES)
 
     def peer(t):
         return ((y + t // 2) % 4) * 2 + (z + t % 2) % 2
@@ -199,8 +199,13 @@
     lax.fori_loop(1, RES, greet, 0)
     for dx in range(1, NX):
         pl.semaphore_signal(barrier, inc=1, device_id=line_id(dx), device_id_type=MESH)
-    for step in (1, -1):
-        pl.semaphore_signal(barrier, inc=1, device_id=sky_id(step), device_id_type=MESH)
+
+    has_next = whole < total_devs - 1
+    has_previous = whole > 0
+    for step, there in ((1, has_next), (-1, has_previous)):
+        @pl.when(there)
+        def _():
+            pl.semaphore_signal(barrier, inc=1, device_id=sky_id(step), device_id_type=MESH)
 
     sci_load += [load_science(q) for q in range(1, NQ)]
     across_load = load(across_hbm, across, 2)
@@ -210,22 +215,14 @@
     start_load.wait()
     starts = (start_ref[0, 0], start_ref[0, 1])
     num[...] = jnp.where(lanes[0:1] == 0, starts[0], starts[1])
-    coef_load.wait()
-    norm_load.wait()
-    tab[...] = jnp.zeros((8, CW), F32)
-    for term in range(3):
-        tab[2 * term : 2 * term + 2, 0:NBASIS] = coef_ref[term]
-    raw = tab[...]
-    weighted = jnp.sum(raw * norm_ref[...], axis=1, keepdims=True)
-    tab[...] = jnp.where(lanes == NBASIS, weighted, raw)
-    tabs[r] = tab[...]
-    nums[r] = num[...]
-
     sky_load.wait()
-    pl.semaphore_wait(barrier, RES - 1 + NX - 1 + 2)
-
-    for side in (0, 1):
-        edge_copy(side).start()
+    ends = (whole + total_devs - 1) // total_devs + (2 * total_devs - 2 - whole) // total_devs
+    pl.semaphore_wait(barrier, RES - 1 + NX - 1 + ends)
+
+    for side, there in ((0, has_next), (1, has_previous)):
+        @pl.when(there)
+        def _():
+            edge_copy(side).start()
     for dx in range(1, NX):
         sky_copy(dx, x).start()
 
@@ -247,6 +244,17 @@
         for e in range(2):
             recv[q][r, e] = chosen(q, r, e)
         if q == 0:
+            coef_load.wait()
+            norm_load.wait()
+            tab[...] = jnp.zeros((8, CW), F32)
+            for term in range(3):
+                tab[2 * term : 2 * term + 2, 0:NBASIS] = coef_ref[term]
+            raw = tab[...]
+            weighted = jnp.sum(raw * norm_ref[...], axis=1, keepdims=True)
+            tab[...] = jnp.where(lanes == NBASIS, weighted, raw)
+            tabs[r] = tab[...]
+            nums[r] = num[...]
+
             def give_tables(i, carry):
                 t = order(i)
                 tab_copy(t, r).start()
@@ -255,8 +263,14 @@
 
             lax.fori_loop(1, RES, give_tables, 0)
         if q == 1:
-            for side in (0, 1):
-                edge_arrival(side).wait_recv()
+            for side, there in ((0, has_previous), (1, has_next)):
+                @pl.when(there)
+                def _():
+                    edge_arrival(side).wait_recv()
+
+                @pl.when(jnp.logical_not(there))
+                def _():
+                    edge[x, side] = jnp.zeros((2 * EDGE, CW), F32)
             for dx in range(1, NX):
                 fwd_copy(dx, x).start()
 
@@ -308,8 +322,6 @@
     sky_copy(1, near).wait_recv()
     spread_across(body_rows(near), [(near, 0, BLK, 0)])
 
-    sky_top = (region == 0) & (r == 0)
-    sky_end = (region == regions - 1) & (r == RES - 1)
     fwd_copy(1, near).wait_recv()
     for side in range(2):
         fwd_copy(1, far + side).wait_recv()
@@ -317,10 +329,6 @@
     for block in range(NX):
         top = edge[block, 0, pl.ds(0, EDGE, stride=2), :]
         low = edge[block, 1, pl.ds(0, EDGE, stride=2), :]
-        if block == 0:
-            top = jnp.where(sky_top, 0.0, top)
-        if block == NX - 1:
-            low = jnp.where(sky_end, 0.0, low)
         rims += [low, top]
     spread_across(
         jnp.concatenate(rims, axis=0), [(block, 2 * EDGE * block, 2 * EDGE, BLK) for block in range(NX)])
@@ -422,8 +430,10 @@
             finish(q - 1)
     finish(NQ - 1)
 
-    for side in (0, 1):
-        edge_copy(side).wait_send()
+    for side, there in ((0, has_next), (1, has_previous)):
+        @pl.when(there)
+        def _():
+            edge_copy(side).wait_send()
     for dx in range(1, NX):
         sky_copy(dx, x).wait_send()
         fwd_copy(dx, x).wait_send()

time: 36.9 us -> 36.9 us (level)
  Pallas kernels: 36.2 us -> 35.8 us
where the time goes in v5:
time: 36.9 us; the launch traced here: 36.5 us
  Pallas kernels  35.8 us (97%)
  local copies, waits for them, and re-layouts  0.66 us (2%)
    pallas_call x1, Pallas kernels, per_device(): pl.pallas_call(lambda *refs: kernel(regions, *refs), out_shape=jax.ShapeD...  35.8 us

profile of v5, /device:TPU:0, one launch (start us, length us, event | category | flops | bytes accessed | tf_op | source)
XLA Modules:
  0.0 36.5 jit_solution(11321918657308527426)
XLA Ops:
  0.0 35.8 %difference_sums.1 = f32[256,128]{1,0:T(8,128)S(1)} custom-call(f32[2,8,256,128]{3,2,1,0:T(8,128)} %bitcast.8, f32[256,128]{1,0:T(8,128)} %bitcast.9, f32[3,2,31]{2,1,0:T(2,128)} %bitcast.10, s32[1,2]{1,0:T(1,128)} %bitcast.11, bf16[6,384,256]{2,1,0:T(8,128)(2,1)} %constant.6.clone.refs_4_, bf16[1536,512]{1,0:T(8,128)(2,1)} %constant.7.clone.refs_5_, ...), custom_call_target="tpu_custom_call" | custom-call | flops 3000000000 | bytes 6000000 | tf_op jit(solution)/shard_map/difference_sums/pallas_call | solution.py:497
  35.8 0.7 %copy.9 = f32[1,128,2,128]{3,2,1,0:T(2,128)} copy(f32[1,128,2,128]{3,2,1,0:T(2,128)S(1)} %bitcast.7) | data formatting | bytes 262144

commit v6 on v5

--- a/solution.py
+++ b/solution.py
@@ -262,7 +262,7 @@
                 return carry
 
             lax.fori_loop(1, RES, give_tables, 0)
-        if q == 1:
+        if q == 2:
             for side, there in ((0, has_previous), (1, has_next)):
                 @pl.when(there)
                 def _():

time: 36.9 us -> 36.8 us (level)
  no operation moved by 1% of the time
where the time goes in v6:
time: 36.8 us; the launch traced here: 36.5 us
  Pallas kernels  35.9 us (98%)
  local copies, waits for them, and re-layouts  0.66 us (2%)
    pallas_call x1, Pallas kernels, per_device(): pl.pallas_call(lambda *refs: kernel(regions, *refs), out_shape=jax.ShapeD...  35.9 us

profile of v6, /device:TPU:0, one launch (start us, length us, event | category | flops | bytes accessed | tf_op | source)
XLA Modules:
  0.0 36.5 jit_solution(18275305670290695447)
XLA Ops:
  0.0 35.9 %difference_sums.1 = f32[256,128]{1,0:T(8,128)S(1)} custom-call(f32[2,8,256,128]{3,2,1,0:T(8,128)} %bitcast.8, f32[256,128]{1,0:T(8,128)} %bitcast.9, f32[3,2,31]{2,1,0:T(2,128)} %bitcast.10, s32[1,2]{1,0:T(1,128)} %bitcast.11, bf16[6,384,256]{2,1,0:T(8,128)(2,1)} %constant.6.clone.refs_4_, bf16[1536,512]{1,0:T(8,128)(2,1)} %constant.7.clone.refs_5_, ...), custom_call_target="tpu_custom_call" | custom-call | flops 3000000000 | bytes 6000000 | tf_op jit(solution)/shard_map/difference_sums/pallas_call | solution.py:497
  35.9 0.7 %copy.9 = f32[1,128,2,128]{3,2,1,0:T(2,128)} copy(f32[1,128,2,128]{3,2,1,0:T(2,128)S(1)} %bitcast.7) | data formatting | bytes 262144
